TPU v7x, 256 devices: a whole 4x4x8 slice. The times are simulated.
256 devices in a mesh: grp: 4 (over y), stretch: 64 (over z, x, core).
Axes of the slice: x: 4, y: 4, z: 8, core: 2. Of those that a mesh axis runs over, the one named last changes fastest.
Arguments:
- queries: bfloat16 [131072, 512], P(('grp', 'stretch')), may hold values from -6 to 6
- keys: bfloat16 [131072, 512], P(('grp', 'stretch')), may hold values from -6 to 6
- values: bfloat16 [131072, 512], P(('grp', 'stretch')), may hold values from -6 to 6
- grad_out: bfloat16 [131072, 512], P(('grp', 'stretch')), may hold values from -6 to 6
- positions: int32 [131072], P(('grp', 'stretch')), may hold values from 0 to 8191, as said below
Outputs:
- grad_queries: bfloat16 [131072, 512], P(('grp', 'stretch'))
- grad_keys: bfloat16 [131072, 512], P(('grp', 'stretch'))
- grad_values: bfloat16 [131072, 512], P(('grp', 'stretch'))
Inputs may be any that keep to these rules, and one draw needn't show every extreme that they name: `positions`: each position is 0 or one more than the position of the token before it; the first token has position 0; no document is longer than min(65536, 8192) tokens, and the last document is exactly that long.
All inputs are finite; a program needn't handle non-finite values.
Results may differ from a plain program's by a relative error of at most 0.006.
Values sent between devices are 32-bit elements; how exact they have to be, the bound alone decides.
No kernel may reach another device: no remote copies, remote signals or barrier semaphores. Data moves between devices by JAX's collectives and lax.ppermute only.
A program may use at most 256 MiB of HBM per device.

v0:
```python
import math

import jax
import jax.numpy as jnp
from jax import lax
from jax.sharding import PartitionSpec as P

HEADS = 4
HEAD_DIM = 128
BLOCK = 512


THETA = 500000.0


def rotary_tables(positions, heads, head_dim):
    half_dim = head_dim // 2
    steps_j = jnp.arange(half_dim, dtype=jnp.float32)
    frequency = jnp.power(jnp.asarray(THETA, jnp.float32), -2.0 * steps_j / head_dim)
    angles = positions.astype(jnp.float32)[:, None] * frequency[None, :]
    cosine = jnp.tile(jnp.cos(angles), (1, 2 * heads))
    sine = jnp.tile(jnp.sin(angles), (1, 2 * heads))
    return (cosine, sine)


def rotate_rows(rows, cosine, sine, heads, head_dim):
    wide = rows.astype(jnp.float32)
    split = wide.reshape(wide.shape[0], heads, 2, head_dim // 2)
    turned = jnp.concatenate([-split[:, :, 1:], split[:, :, :1]], axis=2).reshape(wide.shape)
    return wide * cosine + turned * sine


def unrotate_rows(grads, cosine, sine, heads, head_dim):
    scaled = grads * sine
    split = scaled.reshape(grads.shape[0], heads, 2, head_dim // 2)
    turned = jnp.concatenate([split[:, :, 1:], -split[:, :, :1]], axis=2).reshape(grads.shape)
    return grads * cosine + turned


def shards(queries, keys, values, grad_out, positions):
    rows, width = queries.shape
    count = rows // BLOCK
    f32 = jnp.float32
    total_tokens = rows * lax.axis_size("grp") * lax.axis_size("stretch")
    scale = 1.0 / math.sqrt(HEAD_DIM * total_tokens)
    cosine, sine = rotary_tables(positions, HEADS, HEAD_DIM)
    shape4 = (count, BLOCK, HEADS, HEAD_DIM)
    q_rot = rotate_rows(queries, cosine, sine, HEADS, HEAD_DIM).astype(jnp.bfloat16).reshape(shape4)
    k_rot = rotate_rows(keys, cosine, sine, HEADS, HEAD_DIM).astype(jnp.bfloat16).reshape(shape4)
    v_four = values.reshape(shape4)
    o_four = grad_out.reshape(shape4)
    key_blocks = jnp.einsum("bshd,bshe->bhde", k_rot, v_four, preferred_element_type=f32)
    query_blocks = jnp.einsum("bthd,bthe->bhde", q_rot, o_four, preferred_element_type=f32)
    own_keys = jnp.sum(key_blocks, axis=0)
    own_queries = jnp.sum(query_blocks, axis=0)
    own_pair = jnp.stack([own_keys, own_queries])
    zero_state = jnp.zeros_like(own_keys)
    stretch_index = lax.axis_index("stretch")
    piece = lax.all_gather(own_pair[None], "stretch", axis=0, tiled=True)
    placed = jnp.arange(piece.shape[0])
    before = (placed < stretch_index)[:, None, None, None]
    after = (placed > stretch_index)[:, None, None, None]
    key_prefix = jnp.sum(jnp.where(before, piece[:, 0], 0.0), axis=0)
    query_suffix = jnp.sum(jnp.where(after, piece[:, 1], 0.0), axis=0)
    key_sum = jnp.sum(piece[:, 0], axis=0)
    query_sum = jnp.sum(piece[:, 1], axis=0)
    key_prefix, query_suffix, key_total, query_total = (
        key_prefix,
        query_suffix,
        key_sum,
        query_sum,
    )
    stacked = jnp.stack([key_total, query_total])[None]
    gathered = lax.all_gather(stacked, "grp", axis=0, tiled=True)
    group_index = lax.axis_index("grp")
    order = jnp.arange(gathered.shape[0])[:, None, None, None]
    keys_before = jnp.sum(jnp.where(order < group_index, gathered[:, 0], 0.0), axis=0)
    queries_after = jnp.sum(jnp.where(order > group_index, gathered[:, 1], 0.0), axis=0)
    device_prior = keys_before + key_prefix
    device_later = queries_after + query_suffix
    local_prior = jnp.concatenate([zero_state[None], jnp.cumsum(key_blocks, axis=0)[:-1]], axis=0)
    local_later = jnp.concatenate(
        [jnp.cumsum(query_blocks[::-1], axis=0)[::-1][1:], zero_state[None]], axis=0
    )
    prior_bf = (scale * (device_prior[None] + local_prior)).astype(jnp.bfloat16)
    later_bf = (scale * (device_later[None] + local_later)).astype(jnp.bfloat16)
    lower = jnp.arange(BLOCK)[:, None] >= jnp.arange(BLOCK)[None, :]
    upper = jnp.arange(BLOCK)[:, None] <= jnp.arange(BLOCK)[None, :]
    scores_p = jnp.einsum("bthd,bshd->bhts", o_four, v_four, preferred_element_type=f32)
    weights_p = jnp.where(lower[None, None], scale * scores_p, 0.0).astype(jnp.bfloat16)
    scores_r = jnp.einsum("bshd,bthd->bhst", k_rot, q_rot, preferred_element_type=f32)
    weights_r = jnp.where(upper[None, None], scale * scores_r, 0.0).astype(jnp.bfloat16)
    dq_rot = jnp.einsum("bhts,bshd->bthd", weights_p, k_rot, preferred_element_type=f32)
    dq_rot = dq_rot + jnp.einsum("bthe,bhde->bthd", o_four, prior_bf, preferred_element_type=f32)
    dk_rot = jnp.einsum("bhts,bthd->bshd", weights_p, q_rot, preferred_element_type=f32)
    dk_rot = dk_rot + jnp.einsum("bshe,bhde->bshd", v_four, later_bf, preferred_element_type=f32)
    dv_all = jnp.einsum("bhst,bthe->bshe", weights_r, o_four, preferred_element_type=f32)
    dv_all = dv_all + jnp.einsum("bshd,bhde->bshe", k_rot, later_bf, preferred_element_type=f32)
    grad_queries = unrotate_rows(dq_rot.reshape(rows, width), cosine, sine, HEADS, HEAD_DIM).astype(
        jnp.bfloat16
    )
    grad_keys = unrotate_rows(dk_rot.reshape(rows, width), cosine, sine, HEADS, HEAD_DIM).astype(
        jnp.bfloat16
    )
    grad_values = dv_all.reshape(rows, width).astype(jnp.bfloat16)
    return (grad_queries, grad_keys, grad_values)


def solution(mesh):
    placed = (
        P(("grp", "stretch"), None),
        P(("grp", "stretch"), None),
        P(("grp", "stretch"), None),
        P(("grp", "stretch"), None),
        P(("grp", "stretch")),
    )
    return jax.shard_map(
        shards,
        mesh=mesh,
        in_specs=placed,
        out_specs=(
            P(("grp", "stretch"), None),
            P(("grp", "stretch"), None),
            P(("grp", "stretch"), None),
        ),
        check_vma=False,
    )
```

profile of v0, /device:TPU:1, one launch (start us, length us, event | category | flops | bytes accessed | tf_op | source)
XLA Modules:
  0.0 231.5 jit_solution(2453938085037427536)
XLA Ops:
  7.2 0.0 copy-start
  7.2 0.0 copy-start.1
  7.2 0.0 all-gather.5.cloned.1.call-start
  7.2 1.3 copy.47
  8.5 0.9 slice.51
  9.4 0.1 convert
  9.5 1.3 copy.51
  10.8 0.9 slice.53
  11.6 1.1 convert.1
  12.7 0.0 copy-done.1
  12.7 1.3 copy.73
  14.0 1.1 slice_negate_fusion.2
  15.1 0.5 multiply_cosine_fusion
  15.7 1.4 pad_maximum_fusion
  17.1 0.4 fusion.9
  17.5 0.3 convolution_bitcast_fusion
  17.8 0.0 copy-done
  17.8 0.3 convolution_bitcast_fusion.1
  18.1 0.8 pad_maximum_fusion.4
  18.9 0.0 all-gather.5.cloned.1.call-update
  19.0 0.0 all-gather.7.cloned.1.call-start
  19.0 146.8 %all-gather.5.cloned.1.call-done = f32[128,4,128,128]{3,2,1,0:T(8,128)} async-done(((f32[2,4,128,128]{3,2,1,0:T(8,128)}), f32[128,4,128,128]{3,2,1,0:T(8,128)}) %all-gather.5.cloned.1.call-update) | async-done | bytes 33554448 | tf_op jit(solution)/shard_map/all_gather | solution.py:59
  165.8 11.3 %bitcast_reduce_fusion.1 = (f32[4,128,128]{2,1,0:T(8,128)S(1)}, f32[4,128,128]{2,1,0:T(8,128)S(1)}) fusion(f32[64,2,4,128,128]{4,3,2,1,0:T(8,128)} %bitcast.138), kind=kLoop, calls=%fused_computation.5 | loop fusion | flops 8257536 | bytes 34078720 | tf_op jit(solution)/shard_map/reduce_sum | solution.py:65
  177.2 0.8 pad_maximum_fusion.5
  178.0 0.0 all-gather.7.cloned.1.call-update
  178.1 0.1 iota_compare_fusion.1
  178.1 0.8 iota_compare_fusion
  178.9 0.9 select_convert_fusion.1
  179.8 1.4 fusion.31
  181.3 0.8 fusion.30
  182.1 13.2 %fusion = (f32[4,128,128]{2,1,0:T(8,128)}, f32[4,128,128]{2,1,0:T(8,128)}) fusion(f32[64,2,4,128,128]{4,3,2,1,0:T(8,128)} %bitcast.139, pred[64]{0:T(512)(128)(4,1)S(1)} %get-tuple-element.34, pred[64]{0:T(512)(128)(4,1)S(1)} %get-tuple-element.35), kind=kLoop, calls=%fused_computation.1 | loop fusion | flops 16646144 | bytes 34078848 | tf_op jit(solution)/shard_map/reduce_sum | solution.py:64
  195.3 12.9 %all-gather.7.cloned.1.call-done = f32[8,4,128,128]{3,2,1,0:T(8,128)} async-done(((f32[2,4,128,128]{3,2,1,0:T(8,128)}), f32[8,4,128,128]{3,2,1,0:T(8,128)}) %all-gather.7.cloned.1.call-update) | async-done | bytes 2097168 | tf_op jit(solution)/shard_map/all_gather | solution.py:74
  208.2 2.5 %fusion.15 = (f32[4,128,128]{2,1,0:T(8,128)S(1)}, f32[4,128,128]{2,1,0:T(8,128)}) fusion(f32[4,2,4,128,128]{4,3,2,1,0:T(8,128)} %bitcast.157, pred[4]{0:T(512)(128)(4,1)S(1)} %get-tuple-element.32, pred[4]{0:T(512)(128)(4,1)S(1)} %get-tuple-element.33), kind=kLoop, calls=%fused_computation.32 | loop fusion | flops 917504 | bytes 2621448 | tf_op jit(solution)/shard_map/reduce_sum | solution.py:78
  210.7 1.0 multiply_convert_fusion
  211.7 1.3 fusion.32
  213.0 3.5 %fusion.5 = bf16[4,128,512]{2,1,0:T(8,128)(2,1)} fusion(f32[4,128,512]{2,1,0:T(8,128)} %fusion.32, bf16[512,4,128]{0,2,1:T(8,128)(2,1)S(1)} %bitcast.155, bf16[512,4,128]{0,2,1:T(8,128)(2,1)S(1)} %bitcast.145, bf16[512,4,128]{0,2,1:T(8,128)(2,1)S(1)} %bitcast.152, pred[512,512]{1,0:T(8,128)(4,1)} %iota_compare_fusion), kind=kOutput, calls=%fused_computation.19 | convolution fusion | flops 540540928 | bytes 3407872 | tf_op jit(solution)/shard_map/bhst,bthe->bshe/dot_general | solution.py:97
  216.5 2.0 copy.65
  218.6 1.5 convolution_add_fusion
  220.1 1.3 convolution_add_fusion.1
  221.4 0.2 broadcast_multiply_fusion
  221.7 0.1 fusion.28
  221.8 0.1 fusion.29
  221.9 0.1 pad_maximum_fusion.3
  222.0 0.1 pad_maximum_fusion.2
  222.1 0.6 fusion.13
  222.7 1.0 copy.64
  223.7 1.0 copy.63
  (5 shorter events, 0.1 us)
Async XLA Ops:
  7.2 10.6 %copy-start = (bf16[512,512]{1,0:T(8,128)(2,1)S(1)}, bf16[512,512]{1,0:T(8,128)(2,1)}, u32[]{:S(2)}) copy-start(bf16[512,512]{1,0:T(8,128)(2,1)} %param.7) | copy-start | bytes 1572868
  7.2 5.5 %copy-start.1 = (s32[512]{0:T(512)S(1)}, s32[512]{0:T(512)}, u32[]{:S(2)}) copy-start(s32[512]{0:T(512)} %param.9) | copy-start | bytes 6148
  7.2 158.6 %all-gather.5.cloned.1.call-start = ((), (), s32[]{:S(2)}) async-start(), calls=%async_computation | async-start | bytes 34078720 | tf_op jit(solution)/shard_map/all_gather | solution.py:59
  19.0 189.2 %all-gather.7.cloned.1.call-start = ((), (), s32[]{:S(2)}) async-start(), calls=%async_computation.1 | async-start | bytes 2621440 | tf_op jit(solution)/shard_map/all_gather | solution.py:74
Sparse Core Ops, SparseCore 0:
  19.1 146.6 all-gather.4
  178.1 29.9 all-gather.6
where the time goes:
time: 232 us
  waiting for transfers between devices  160 us (69%)
  other arithmetic  36.6 us (16%)
  between operations  14.2 us (6%)
  matrix products  11.4 us (5%)
  local copies, waits for them, and re-layouts  9.54 us (4%)
    all_gather x1, waiting for transfers between devices, shards(): piece = lax.all_gather(own_pair[None], 'stretch', axis=0, tiled=True)  147 us
    reduce_sum x1, other arithmetic, shards(): query_suffix = jnp.sum(jnp.where(after, piece[:, 1], 0.0), axis=0)  13.2 us
    all_gather x1, waiting for transfers between devices, shards(): gathered = lax.all_gather(stacked, 'grp', axis=0, tiled=True)  12.9 us
    reduce_sum x1, other arithmetic, shards(): key_sum = jnp.sum(piece[:, 0], axis=0)  11.3 us
    unnamed x9, local copies, waits for them, and re-layouts  6.58 us
  transfers between devices with their start and end apart: 2, of which 2 were waited for; matrix products, arithmetic and copies ran while one was open for 7% of the time, Pallas kernels for 0%

commit v1 on v0

v1 whole, which is shorter than its diff:
```python
import math

import numpy as np
import jax
import jax.numpy as jnp
from jax import lax
from jax.experimental import pallas as pl
from jax.experimental.pallas import tpu as pltpu
from jax.sharding import Mesh, PartitionSpec as P

HEADS = 4
HEAD_DIM = 128
BLOCK = 512
THETA = 500000.0
WIDTH = HEADS * HEAD_DIM
HALF = HEAD_DIM // 2
F32 = jnp.float32
BF16 = jnp.bfloat16
VMEM_LIMIT = 48 * 1024 * 1024
WHOLE = pl.BlockSpec(memory_space=pltpu.VMEM)
SCALAR = pl.BlockSpec(memory_space=pltpu.SMEM)

FREQUENCY = np.tile(
    np.power(THETA, -2.0 * np.arange(HALF) / HEAD_DIM), 2
).astype(np.float32)[None, :]

HALF_PI = (1.5703125, 4.837512969970703125e-4, 7.54978995489188216e-8)


def params():
    return pltpu.CompilerParams(vmem_limit_bytes=VMEM_LIMIT)


def sin_cos(angle):
    turns = jnp.floor(angle * (2.0 / math.pi) + 0.5)
    r = angle - turns * HALF_PI[0]
    r = r - turns * HALF_PI[1]
    r = r - turns * HALF_PI[2]
    r2 = r * r
    s = r + r * r2 * (-1.6666654611e-1 + r2 * (8.3321608736e-3 + r2 * -1.9515295891e-4))
    c = 1.0 + r2 * (-0.5 + r2 * (4.166664568298827e-2 + r2 * (-1.388731625493765e-3 + r2 * 2.443315711809948e-5)))
    quadrant = turns.astype(jnp.int32) & 3
    odd = (quadrant & 1) == 1
    sine = jnp.where(odd, c, s)
    cosine = jnp.where(odd, s, c)
    sine = jnp.where(quadrant >= 2, -sine, sine)
    cosine = jnp.where((quadrant == 1) | (quadrant == 2), -cosine, cosine)
    return sine, cosine


def dot(a, b, dims):
    return lax.dot_general(a, b, (dims, ((), ())), preferred_element_type=F32)


def head(ref, h):
    return ref[:, h * HEAD_DIM : (h + 1) * HEAD_DIM]


def rotate_kernel(core_ref, pos_ref, freq_ref, q_ref, k_ref, v_ref, o_ref, qr_ref, kr_ref, cos_ref, sin_ref, mine_ref, other_ref):
    core = core_ref[0]
    first = lax.broadcasted_iota(jnp.int32, (HEAD_DIM, HEAD_DIM), 1) < HALF
    for i in range(BLOCK // HEAD_DIM):
        row = jnp.broadcast_to(pos_ref[i : i + 1, :].astype(F32), (HEAD_DIM, HEAD_DIM))
        sine, cosine = sin_cos(row.T * freq_ref[...])
        rows = slice(i * HEAD_DIM, (i + 1) * HEAD_DIM)
        cos_ref[rows, :] = cosine
        sin_ref[rows, :] = jnp.where(first, -sine, sine)
    for h in range(HEADS):
        cosine, sine = cos_ref[...], sin_ref[...]
        cols = slice(h * HEAD_DIM, (h + 1) * HEAD_DIM)
        q = head(q_ref, h).astype(F32)
        qr = (q * cosine + pltpu.roll(q, HALF, 1) * sine).astype(BF16)
        qr_ref[:, cols] = qr
        k = head(k_ref, h).astype(F32)
        kr = (k * cosine + pltpu.roll(k, HALF, 1) * sine).astype(BF16)
        kr_ref[:, cols] = kr
        key_state = dot(kr, head(v_ref, h), ((0,), (0,)))
        query_state = dot(qr, head(o_ref, h), ((0,), (0,)))
        rows = slice(h * HEAD_DIM, (h + 1) * HEAD_DIM)
        mine_ref[rows, :] = jnp.where(core == 0, key_state, query_state)
        other_ref[rows, :] = jnp.where(core == 0, query_state, key_state)


def intra_kernel(qr_ref, kr_ref, v_ref, o_ref, dq_ref, dk_ref, dv_ref):
    n = BLOCK // 2
    row = lax.broadcasted_iota(jnp.int32, (n, n), 0)
    col = lax.broadcasted_iota(jnp.int32, (n, n), 1)
    lower = row >= col
    upper = row <= col
    top, low = slice(0, n), slice(n, BLOCK)
    lanes = ((1,), (1,))
    plain = ((1,), (0,))
    for h in range(HEADS):
        cols = slice(h * HEAD_DIM, (h + 1) * HEAD_DIM)
        q1, q2 = qr_ref[top, cols], qr_ref[low, cols]
        k1, k2 = kr_ref[top, cols], kr_ref[low, cols]
        v1, v2 = v_ref[top, cols], v_ref[low, cols]
        o1, o2 = o_ref[top, cols], o_ref[low, cols]

        def score(a, b, mask=None):
            s = dot(a, b, lanes)
            return (s if mask is None else jnp.where(mask, s, 0.0)).astype(BF16)

        dq_ref[top, cols] = dot(score(o1, v1, lower), k1, plain)
        dq_ref[low, cols] = dot(score(o2, v1), k1, plain) + dot(score(o2, v2, lower), k2, plain)
        dk_ref[top, cols] = dot(score(v1, o1, upper), q1, plain) + dot(score(v1, o2), q2, plain)
        dk_ref[low, cols] = dot(score(v2, o2, upper), q2, plain)
        dv_ref[top, cols] = dot(score(k1, q1, upper), o1, plain) + dot(score(k1, q2), o2, plain)
        dv_ref[low, cols] = dot(score(k2, q2, upper), o2, plain)


def scan_kernel(core_ref, r_ref, total_ref, pre_ref):
    n = r_ref.shape[0]
    total = r_ref[0]
    for i in range(1, n):
        total = total + r_ref[i]
    total_ref[...] = total
    up = core_ref[0] == 0

    @pl.when(up)
    def _():
        acc = jnp.zeros_like(total)
        for i in range(n):
            pre_ref[i] = acc
            acc = acc + r_ref[i]

    @pl.when(jnp.logical_not(up))
    def _():
        acc = jnp.zeros_like(total)
        for i in reversed(range(n)):
            pre_ref[i] = acc
            acc = acc + r_ref[i]


def final_kernel(core_ref, chip_ref, recv_ref, kr_ref, v_ref, o_ref, cos_ref, sin_ref, dq_ref, dk_ref, dv_ref, gq_ref, gk_ref, gv_ref, *, scale):
    core = core_ref[0]
    cosine = cos_ref[...] * scale
    sine = sin_ref[...] * scale
    for h in range(HEADS):
        cols = slice(h * HEAD_DIM, (h + 1) * HEAD_DIM)
        rows = slice(h * HEAD_DIM, (h + 1) * HEAD_DIM)
        chip, recv = chip_ref[rows, :], recv_ref[rows, :]
        prior = jnp.where(core == 0, chip, recv).astype(BF16)
        later = jnp.where(core == 0, recv, chip).astype(BF16)
        dq = dq_ref[:, cols] + dot(o_ref[:, cols], prior, ((1,), (1,)))
        gq_ref[:, cols] = (dq * cosine - pltpu.roll(dq, HALF, 1) * sine).astype(BF16)
        dk = dk_ref[:, cols] + dot(v_ref[:, cols], later, ((1,), (1,)))
        gk_ref[:, cols] = (dk * cosine - pltpu.roll(dk, HALF, 1) * sine).astype(BF16)
        dv = dv_ref[:, cols] + dot(kr_ref[:, cols], later, ((1,), (0,)))
        gv_ref[:, cols] = (dv * scale).astype(BF16)


def call(kernel, outs, in_specs, cost):
    return pl.pallas_call(
        kernel,
        out_shape=tuple(jax.ShapeDtypeStruct(s, d) for s, d in outs),
        in_specs=in_specs,
        out_specs=tuple(WHOLE for _ in outs),
        compiler_params=params(),
        cost_estimate=pl.CostEstimate(flops=cost[0], bytes_accessed=cost[1], transcendentals=0),
    )


def shards(queries, keys, values, grad_out, positions):
    ny, nz, nx = lax.axis_size("y"), lax.axis_size("z"), lax.axis_size("x")
    scale = 1.0 / math.sqrt(HEAD_DIM * BLOCK * ny * nz * nx * 2)
    core = lax.axis_index("core")
    core_s = core.astype(jnp.int32)[None]
    wide, state = (BLOCK, WIDTH), (WIDTH, HEAD_DIM)
    qr, kr, cosine, sine, mine, other = call(
        rotate_kernel,
        [(wide, BF16), (wide, BF16), ((BLOCK, HEAD_DIM), F32), ((BLOCK, HEAD_DIM), F32), (state, F32), (state, F32)],
        [SCALAR] + [WHOLE] * 6,
        (2 * 8 * 512 * 128 * 128, 4 << 20),
    )(core_s, positions.reshape(BLOCK // HEAD_DIM, HEAD_DIM), jnp.asarray(FREQUENCY), queries, keys, values, grad_out)

    swap = [(0, 1), (1, 0)]
    chips = nz * nx
    piece = (WIDTH // chips, HEAD_DIM)
    pair = mine + lax.ppermute(other, "core", swap)
    pieces = lax.all_to_all(pair.reshape((chips,) + piece), ("z", "x"), 0, 0)
    total, pre = call(
        scan_kernel, [(piece, F32), ((chips,) + piece, F32)], [SCALAR, WHOLE], (0, 1 << 19)
    )(core_s, pieces)
    y = lax.axis_index("y")
    above = jnp.zeros(piece, F32)
    for step in range(1, ny):
        came = lax.ppermute(total, "y", [(i, (i + step) % ny) for i in range(ny)])
        origin = lax.rem(y - step + ny, ny)
        wanted = jnp.where(core == 0, origin < y, origin > y)
        above = above + jnp.where(wanted, came, 0.0)
    dq, dk, dv = call(
        intra_kernel, [(wide, F32)] * 3, [WHOLE] * 4, (2 * 4 * 6 * 512 * 512 * 128, 5 << 20)
    )(qr, kr, values, grad_out)
    chip = lax.all_to_all(pre + above[None], ("z", "x"), 0, 0).reshape(state)
    came = lax.ppermute(chip + mine, "core", swap)

    def final(*refs):
        final_kernel(*refs, scale=scale)

    return call(
        final, [(wide, BF16)] * 3, [SCALAR] + [WHOLE] * 10, (2 * 4 * 3 * 512 * 128 * 128, 7 << 20)
    )(core_s, chip, came, kr, values, grad_out, cosine, sine, dq, dk, dv)


def solution(mesh):
    ny = mesh.shape["grp"]
    nz, nx = 8, 4
    fine = Mesh(mesh.devices.reshape(ny, nz, nx, 2), ("y", "z", "x", "core"))
    every = ("y", "z", "x", "core")
    return jax.shard_map(
        shards,
        mesh=fine,
        in_specs=(P(every, None),) * 4 + (P(every),),
        out_specs=(P(every, None),) * 3,
        check_vma=False,
    )
```

time: 232 us -> 65.8 us (0.28)
  waiting for transfers between devices: 160 us -> 4.22 us
  other arithmetic: 36.6 us -> 0.1 us
  blocking collectives: 0 us -> 35.7 us
  between operations: 14.2 us -> 0.71 us
  starting transfers between devices: 0.08 us -> 11.9 us
  matrix products: 11.4 us -> 0 us
  Pallas kernels: 0 us -> 7.98 us
  local copies, waits for them, and re-layouts: 9.54 us -> 4.84 us
    all_gather x2 -> x0, waiting for transfers between devices: 160 us -> none  [the longest x1 147 us: shards(): piece = lax.all_gather(own_pair[None], 'stretch', axis=0, tiled=True)]
    all_to_all x0 -> x2, blocking collectives: none -> 35.7 us  [the longest x1 20.7 us: shards(): pieces = lax.all_to_all(pair.reshape((chips,) + piece), ('z', 'x'), 0, 0)]
    reduce_sum x3 -> x0, other arithmetic: 27.1 us -> none  [the longest x1 13.2 us: shards(): query_suffix = jnp.sum(jnp.where(after, piece[:, 1], 0.0), axis=0)]
    ppermute x0 -> x5, starting transfers between devices: none -> 11.9 us  [the longest x1 4.68 us: shards(): came = lax.ppermute(chip + mine, 'core', swap)]
    dot_general x9 -> x0, matrix products: 11.4 us -> none  [the longest x1 3.48 us: shards(): jnp.einsum('bhst,bthe->bshe', weights_r, o_four, preferred_element_type=f32)]
    pallas_call x0 -> x4, Pallas kernels: none -> 7.98 us  [the longest x1 4.18 us: shards(): call(intra_kernel, [(wide, F32)] * 3, [WHOLE] * 4, (2 * 4 * 6 * 512 * 512...]
    ppermute x0 -> x5, waiting for transfers between devices: none -> 4.22 us  [the longest x3 3.05 us: shards(): came = lax.ppermute(total, 'y', [(i, (i + step) % ny) for i in range(ny)])]
    unnamed x9 -> x16, local copies, waits for them, and re-layouts: 6.58 us -> 4.84 us
  transfers between devices with their start and end apart: 2 -> 5, of which waited for: 2 -> 3; matrix products, arithmetic and copies ran while one was open for 7% -> 0% of each run, Pallas kernels for 0% -> 6%
where the time goes in v1:
time: 65.8 us; the launch traced here: 65.4 us
  blocking collectives  35.7 us (54%)
  starting transfers between devices  11.9 us (18%)
  Pallas kernels  7.98 us (12%)
  local copies, waits for them, and re-layouts  4.84 us (7%)
  waiting for transfers between devices  4.22 us (6%)
  between operations  0.71 us (1%)
    all_to_all x1, blocking collectives, shards(): pieces = lax.all_to_all(pair.reshape((chips,) + piece), ('z', 'x'), 0, 0)  20.7 us
    all_to_all x1, blocking collectives, shards(): chip = lax.all_to_all(pre + above[None], ('z', 'x'), 0, 0).reshape(state)  15 us
    unnamed x16, local copies, waits for them, and re-layouts  4.84 us
    ppermute x1, starting transfers between devices, shards(): came = lax.ppermute(chip + mine, 'core', swap)  4.68 us
    pallas_call x1, Pallas kernels, shards(): call(intra_kernel, [(wide, F32)] * 3, [WHOLE] * 4, (2 * 4 * 6 * 512 * 512...  4.18 us
    ppermute x3, starting transfers between devices, shards(): came = lax.ppermute(total, 'y', [(i, (i + step) % ny) for i in range(ny)])  3.85 us
    ppermute x1, starting transfers between devices, shards(): pair = mine + lax.ppermute(other, 'core', swap)  3.33 us
    ppermute x3, waiting for transfers between devices, shards(): came = lax.ppermute(total, 'y', [(i, (i + step) % ny) for i in range(ny)])  3.05 us
  transfers between devices with their start and end apart: 5, of which 3 were waited for; matrix products, arithmetic and copies ran while one was open for 0% of the time, Pallas kernels for 6%

profile of v1, /device:TPU:1, one launch (start us, length us, event | category | flops | bytes accessed | tf_op | source)
XLA Modules:
  0.0 65.4 jit_solution(18437030867538575197)
XLA Ops:
  0.6 0.0 copy-start.6
  0.6 0.0 copy-start.7
  0.7 0.7 %copy-done.6 = s32[512]{0:T(512)S(1)} copy-done((s32[512]{0:T(512)S(1)}, s32[512]{0:T(512)}, u32[]{:S(2)}) %copy-start.6) | copy-done | bytes 2072
  1.3 0.0 copy-done.7
  1.3 0.0 copy-start
  1.3 1.0 %copy-done = bf16[512,512]{1,0:T(8,128)(2,1)S(1)} copy-done((bf16[512,512]{1,0:T(8,128)(2,1)S(1)}, bf16[512,512]{1,0:T(8,128)(2,1)}, u32[]{:S(2)}) %copy-start) | copy-done | bytes 524312
  2.4 0.0 copy-start.2
  2.4 1.0 %copy-done.2 = bf16[512,512]{1,0:T(8,128)(2,1)S(1)} copy-done((bf16[512,512]{1,0:T(8,128)(2,1)S(1)}, bf16[512,512]{1,0:T(8,128)(2,1)}, u32[]{:S(2)}) %copy-start.2) | copy-done | bytes 524312
  3.4 0.0 copy-start.4
  3.4 1.0 %copy-done.4 = bf16[512,512]{1,0:T(8,128)(2,1)S(1)} copy-done((bf16[512,512]{1,0:T(8,128)(2,1)S(1)}, bf16[512,512]{1,0:T(8,128)(2,1)}, u32[]{:S(2)}) %copy-start.4) | copy-done | bytes 524312
  4.4 0.0 copy-start.5
  4.5 1.0 %copy-done.5 = bf16[512,512]{1,0:T(8,128)(2,1)S(1)} copy-done((bf16[512,512]{1,0:T(8,128)(2,1)S(1)}, bf16[512,512]{1,0:T(8,128)(2,1)}, u32[]{:S(2)}) %copy-start.5) | copy-done | bytes 524312
  5.5 1.5 %shard_map.85 = (bf16[512,512]{1,0:T(8,128)(2,1)S(1)}, bf16[512,512]{1,0:T(8,128)(2,1)S(1)}, f32[512,128]{1,0:T(8,128)S(1)}, f32[512,128]{1,0:T(8,128)S(1)}, f32...) custom-call(s32[1]{0:T(128)} %bitcast.core_ref.refs_0_, s32[4,128]{1,0:T(4,128)S(1)} %bitcast.6, f32[1,128]{1,0:T(1,128)S(1)} %copy-done.7, ...), custom_call_target="tpu_custom_call" | custom-call | flops 134217728 | bytes 4194304 | tf_op jit(solution)/shard_map/pallas_call | solution.py:170
  7.0 3.3 %collective-permute-start = (f32[512,128]{1,0:T(8,128)S(1)}, f32[512,128]{1,0:T(8,128)S(1)}, u32[]{:S(2)}, u32[]{:S(2)}) collective-permute-start(f32[512,128]{1,0:T(8,128)S(1)} %get-tuple-element.15), channel_id=1, source_target_pairs={{0,1},{1,0},{2,3},{3,2},{4,5},{5,4},{6,7},{7,6},{8,9},{9,8},{10,11... | collective-permute-start | bytes 786440 | tf_op jit(solution)/shard_map/ppermute | solution.py:180
  10.3 1.2 %collective-permute-done = f32[512,128]{1,0:T(8,128)S(1)} collective-permute-done((f32[512,128]{1,0:T(8,128)S(1)}, f32[512,128]{1,0:T(8,128)S(1)}, u32[]{:S(2)}, u32[]{:S(2)}) %collective-permute-start) | collective-permute-done | bytes 262176 | tf_op jit(solution)/shard_map/ppermute | solution.py:180
  11.5 20.7 %all_to_all.10.r_ref = f32[32,16,128]{2,1,0:T(8,128)S(1)} all-to-all(f32[32,16,128]{2,1,0:T(8,128)S(1)} %bitcast.7), channel_id=1, replica_groups=mesh['y'=4,'z'=8,'x'=4,'core'=2] {'z','x'}, dimensions={0} | all-to-all | bytes 524288 | tf_op jit(solution)/shard_map/all_to_all | solution.py:181
  32.2 0.1 shard_map.86
  32.3 2.8 %collective-permute-start.3 = (f32[16,128]{1,0:T(8,128)S(1)}, f32[16,128]{1,0:T(8,128)S(1)}, u32[]{:S(2)}, u32[]{:S(2)}) collective-permute-start(f32[16,128]{1,0:T(8,128)S(1)} %get-tuple-element.17), channel_id=1, source_target_pairs={{0,192},{64,0},{128,64},{192,128},{1,193},{65,1},{129,65},{193,129... | collective-permute-start | bytes 24584 | tf_op jit(solution)/shard_map/ppermute | solution.py:188
  35.1 0.3 collective-permute-start.2
  35.4 0.7 %collective-permute-start.1 = (f32[16,128]{1,0:T(8,128)S(1)}, f32[16,128]{1,0:T(8,128)S(1)}, u32[]{:S(2)}, u32[]{:S(2)}) collective-permute-start(f32[16,128]{1,0:T(8,128)S(1)} %get-tuple-element.17), channel_id=1, source_target_pairs={{0,64},{64,128},{128,192},{192,0},{1,65},{65,129},{129,193},{193,1... | collective-permute-start | bytes 24584 | tf_op jit(solution)/shard_map/ppermute | solution.py:188
  36.1 0.0 collective-permute-done.3
  36.1 3.0 %collective-permute-done.2 = f32[16,128]{1,0:T(8,128)S(1)} collective-permute-done((f32[16,128]{1,0:T(8,128)S(1)}, f32[16,128]{1,0:T(8,128)S(1)}, u32[]{:S(2)}, u32[]{:S(2)}) %collective-permute-start.2) | collective-permute-done | bytes 8224 | tf_op jit(solution)/shard_map/ppermute | solution.py:188
  39.1 0.1 collective-permute-done.1
  39.2 0.0 copy-start.3
  39.2 15.0 %all_to_all.11 = f32[32,16,128]{2,1,0:T(8,128)S(1)} all-to-all(f32[32,16,128]{2,1,0:T(8,128)S(1)} %broadcast_add_fusion), channel_id=1, replica_groups=mesh['y'=4,'z'=8,'x'=4,'core'=2] {'z','x'}, dimensions={0} | all-to-all | bytes 524288 | tf_op jit(solution)/shard_map/all_to_all | solution.py:195
  54.2 0.0 copy-start.1
  54.2 4.7 %collective-permute-start.4 = (f32[512,128]{1,0:T(8,128)S(1)}, f32[512,128]{1,0:T(8,128)S(1)}, u32[]{:S(2)}, u32[]{:S(2)}) collective-permute-start(f32[512,128]{1,0:T(8,128)S(1)} %bitcast_add_fusion), channel_id=1, source_target_pairs={{0,1},{1,0},{2,3},{3,2},{4,5},{5,4},{6,7},{7,6},{8,9},{9,8},{10,11... | collective-permute-start | bytes 786440 | tf_op jit(solution)/shard_map/ppermute | solution.py:196
  58.9 0.0 copy-done.3
  58.9 0.0 copy-done.1
  58.9 4.2 %shard_map.87 = (f32[512,512]{1,0:T(8,128)S(1)}, f32[512,512]{1,0:T(8,128)S(1)}, f32[512,512]{1,0:T(8,128)S(1)}) custom-call(bf16[512,512]{1,0:T(8,128)(2,1)S(1)} %get-tuple-element.21.qr_ref, bf16[512,512]{1,0:T(8,128)(2,1)S(1)} %get-tuple-element.18.kr_ref.refs_3_, bf16[512,512]{1,0:T(8,128)(2,1)S(1)} %copy-done.1, bf16[512,512]{1,0:T(8,128)(2,1)S(1)} %copy-done.3), custom_call_target="tpu_custom_call" | custom-call | flops 1610612736 | bytes 5242880 | tf_op jit(solution)/shard_map/pallas_call | solution.py:192
  63.1 0.0 collective-permute-done.4.refs_2_
  63.1 2.3 %shard_map.88 = (bf16[512,512]{1,0:T(8,128)(2,1)}, bf16[512,512]{1,0:T(8,128)(2,1)}, bf16[512,512]{1,0:T(8,128)(2,1)}) custom-call(s32[1]{0:T(128)} %bitcast.core_ref.refs_0_, f32[512,128]{1,0:T(8,128)S(1)} %bitcast.5, f32[512,128]{1,0:T(8,128)S(1)} %collective-permute-done.4.refs_2_, bf16[512,512]{1,0:T(8,128)(2,1)S(1)} %get-tuple-element.18.kr_ref.refs_3_, ...), custom_call_target="tpu_custom_call" | custom-call | flops 201326592 | bytes 7340032 | tf_op jit(solution)/shard_map/pallas_call | solution.py:201
  (4 shorter events, 0.1 us)
Async XLA Ops:
  0.6 0.7 %copy-start.6 = (s32[512]{0:T(512)S(1)}, s32[512]{0:T(512)}, u32[]{:S(2)}) copy-start(s32[512]{0:T(512)} %param.10) | copy-start | bytes 6148
  0.6 0.7 %copy-start.7 = (f32[1,128]{1,0:T(1,128)S(1)}, f32[1,128]{1,0:T(1,128)}, u32[]{:S(2)}) copy-start(f32[1,128]{1,0:T(1,128)} %constant.35.clone.freq_ref) | copy-start | bytes 1540
  1.3 1.0 %copy-start = (bf16[512,512]{1,0:T(8,128)(2,1)S(1)}, bf16[512,512]{1,0:T(8,128)(2,1)}, u32[]{:S(2)}) copy-start(bf16[512,512]{1,0:T(8,128)(2,1)} %refs_4_.1) | copy-start | bytes 1572868
  2.4 1.0 %copy-start.2 = (bf16[512,512]{1,0:T(8,128)(2,1)S(1)}, bf16[512,512]{1,0:T(8,128)(2,1)}, u32[]{:S(2)}) copy-start(bf16[512,512]{1,0:T(8,128)(2,1)} %refs_5_.1) | copy-start | bytes 1572868
  3.4 1.0 %copy-start.4 = (bf16[512,512]{1,0:T(8,128)(2,1)S(1)}, bf16[512,512]{1,0:T(8,128)(2,1)}, u32[]{:S(2)}) copy-start(bf16[512,512]{1,0:T(8,128)(2,1)} %q_ref.1) | copy-start | bytes 1572868
  4.4 1.0 %copy-start.5 = (bf16[512,512]{1,0:T(8,128)(2,1)S(1)}, bf16[512,512]{1,0:T(8,128)(2,1)}, u32[]{:S(2)}) copy-start(bf16[512,512]{1,0:T(8,128)(2,1)} %k_ref.1) | copy-start | bytes 1572868
  7.0 4.5 %collective-permute-start = (f32[512,128]{1,0:T(8,128)S(1)}, f32[512,128]{1,0:T(8,128)S(1)}, u32[]{:S(2)}, u32[]{:S(2)}) collective-permute-start(f32[512,128]{1,0:T(8,128)S(1)} %get-tuple-element.15), channel_id=1, source_target_pairs={{0,1},{1,0},{2,3},{3,2},{4,5},{5,4},{6,7},{7,6},{8,9},{9,8},{10,11... | collective-permute-start | bytes 786440 | tf_op jit(solution)/shard_map/ppermute | solution.py:180
  32.3 3.9 %collective-permute-start.3 = (f32[16,128]{1,0:T(8,128)S(1)}, f32[16,128]{1,0:T(8,128)S(1)}, u32[]{:S(2)}, u32[]{:S(2)}) collective-permute-start(f32[16,128]{1,0:T(8,128)S(1)} %get-tuple-element.17), channel_id=1, source_target_pairs={{0,192},{64,0},{128,64},{192,128},{1,193},{65,1},{129,65},{193,129... | collective-permute-start | bytes 24584 | tf_op jit(solution)/shard_map/ppermute | solution.py:188
  35.1 4.0 %collective-permute-start.2 = (f32[16,128]{1,0:T(8,128)S(1)}, f32[16,128]{1,0:T(8,128)S(1)}, u32[]{:S(2)}, u32[]{:S(2)}) collective-permute-start(f32[16,128]{1,0:T(8,128)S(1)} %get-tuple-element.17), channel_id=1, source_target_pairs={{0,128},{64,192},{128,0},{192,64},{1,129},{65,193},{129,1},{193,65... | collective-permute-start | bytes 24584 | tf_op jit(solution)/shard_map/ppermute | solution.py:188
  35.4 3.7 %collective-permute-start.1 = (f32[16,128]{1,0:T(8,128)S(1)}, f32[16,128]{1,0:T(8,128)S(1)}, u32[]{:S(2)}, u32[]{:S(2)}) collective-permute-start(f32[16,128]{1,0:T(8,128)S(1)} %get-tuple-element.17), channel_id=1, source_target_pairs={{0,64},{64,128},{128,192},{192,0},{1,65},{65,129},{129,193},{193,1... | collective-permute-start | bytes 24584 | tf_op jit(solution)/shard_map/ppermute | solution.py:188
  39.2 19.7 %copy-start.3 = (bf16[512,512]{1,0:T(8,128)(2,1)S(1)}, bf16[512,512]{1,0:T(8,128)(2,1)}, u32[]{:S(2)}) copy-start(bf16[512,512]{1,0:T(8,128)(2,1)} %refs_5_.1) | copy-start | bytes 1572868
  54.2 4.7 %copy-start.1 = (bf16[512,512]{1,0:T(8,128)(2,1)S(1)}, bf16[512,512]{1,0:T(8,128)(2,1)}, u32[]{:S(2)}) copy-start(bf16[512,512]{1,0:T(8,128)(2,1)} %refs_4_.1) | copy-start | bytes 1572868
  54.2 8.9 %collective-permute-start.4 = (f32[512,128]{1,0:T(8,128)S(1)}, f32[512,128]{1,0:T(8,128)S(1)}, u32[]{:S(2)}, u32[]{:S(2)}) collective-permute-start(f32[512,128]{1,0:T(8,128)S(1)} %bitcast_add_fusion), channel_id=1, source_target_pairs={{0,1},{1,0},{2,3},{3,2},{4,5},{5,4},{6,7},{7,6},{8,9},{9,8},{10,11... | collective-permute-start | bytes 786440 | tf_op jit(solution)/shard_map/ppermute | solution.py:196

commit v2 on v1

v2 whole, which is shorter than its diff:
```python
import math

import numpy as np
import jax
import jax.numpy as jnp
from jax import lax
from jax.experimental import pallas as pl
from jax.experimental.pallas import tpu as pltpu
from jax.sharding import Mesh, PartitionSpec as P

HEADS = 4
HEAD_DIM = 128
BLOCK = 512
THETA = 500000.0
WIDTH = HEADS * HEAD_DIM
HALF = HEAD_DIM // 2
F32 = jnp.float32
BF16 = jnp.bfloat16
VMEM_LIMIT = 48 * 1024 * 1024
WHOLE = pl.BlockSpec(memory_space=pltpu.VMEM)
HBM = pl.BlockSpec(memory_space=pltpu.HBM)
SCALAR = pl.BlockSpec(memory_space=pltpu.SMEM)

FREQUENCY = np.tile(
    np.power(THETA, -2.0 * np.arange(HALF) / HEAD_DIM), 2
).astype(np.float32)[None, :]

HALF_PI = (1.5703125, 4.837512969970703125e-4, 7.54978995489188216e-8)


def params():
    return pltpu.CompilerParams(vmem_limit_bytes=VMEM_LIMIT)


def sin_cos(angle):
    turns = jnp.floor(angle * (2.0 / math.pi) + 0.5)
    r = angle - turns * HALF_PI[0]
    r = r - turns * HALF_PI[1]
    r = r - turns * HALF_PI[2]
    r2 = r * r
    s = r + r * r2 * (-1.6666654611e-1 + r2 * (8.3321608736e-3 + r2 * -1.9515295891e-4))
    c = 1.0 + r2 * (-0.5 + r2 * (4.166664568298827e-2 + r2 * (-1.388731625493765e-3 + r2 * 2.443315711809948e-5)))
    quadrant = turns.astype(jnp.int32) & 3
    odd = (quadrant & 1) == 1
    sine = jnp.where(odd, c, s)
    cosine = jnp.where(odd, s, c)
    sine = jnp.where(quadrant >= 2, -sine, sine)
    cosine = jnp.where((quadrant == 1) | (quadrant == 2), -cosine, cosine)
    return sine, cosine


def dot(a, b, dims):
    return lax.dot_general(a, b, (dims, ((), ())), preferred_element_type=F32)


def rotate_kernel(
    core_ref, pos_hbm, freq_hbm, q_hbm, k_hbm, v_hbm, o_hbm,
    qr_ref, kr_ref, v_ref, o_ref, cos_ref, sin_ref, mine_ref, other_ref,
    pos_ref, freq_ref, q_ref, k_ref, small_sems, sems,
):
    core = core_ref[0]
    small = [
        pltpu.make_async_copy(pos_hbm, pos_ref, small_sems.at[0]),
        pltpu.make_async_copy(freq_hbm, freq_ref, small_sems.at[1]),
    ]
    for copy in small:
        copy.start()
    copies = []
    for h in range(HEADS):
        cols = slice(h * HEAD_DIM, (h + 1) * HEAD_DIM)
        pairs = ((k_hbm, k_ref), (v_hbm, v_ref), (q_hbm, q_ref), (o_hbm, o_ref))
        of_head = [
            pltpu.make_async_copy(src.at[:, cols], dst.at[:, cols], sems.at[4 * h + i])
            for i, (src, dst) in enumerate(pairs)
        ]
        for copy in of_head:
            copy.start()
        copies.append(of_head)
    first = lax.broadcasted_iota(jnp.int32, (HEAD_DIM, HEAD_DIM), 1) < HALF
    for copy in small:
        copy.wait()
    for i in range(BLOCK // HEAD_DIM):
        row = jnp.broadcast_to(pos_ref[i : i + 1, :].astype(F32), (HEAD_DIM, HEAD_DIM))
        sine, cosine = sin_cos(row.T * freq_ref[...])
        rows = slice(i * HEAD_DIM, (i + 1) * HEAD_DIM)
        cos_ref[rows, :] = cosine
        sin_ref[rows, :] = jnp.where(first, -sine, sine)
    for h in range(HEADS):
        for copy in copies[h]:
            copy.wait()
        cosine, sine = cos_ref[...], sin_ref[...]
        cols = slice(h * HEAD_DIM, (h + 1) * HEAD_DIM)
        rows = cols
        k = k_ref[:, cols].astype(F32)
        kr = (k * cosine + pltpu.roll(k, HALF, 1) * sine).astype(BF16)
        kr_ref[:, cols] = kr
        key_state = dot(kr, v_ref[:, cols], ((0,), (0,)))
        q = q_ref[:, cols].astype(F32)
        qr = (q * cosine + pltpu.roll(q, HALF, 1) * sine).astype(BF16)
        qr_ref[:, cols] = qr
        query_state = dot(qr, o_ref[:, cols], ((0,), (0,)))
        mine_ref[rows, :] = jnp.where(core == 0, key_state, query_state)
        other_ref[rows, :] = jnp.where(core == 0, query_state, key_state)


def lower_kernel(a_ref, b_ref, c_ref, out_ref):
    triangle_kernel(a_ref, b_ref, c_ref, out_ref, True)


def upper_kernel(a_ref, b_ref, c_ref, out_ref):
    triangle_kernel(a_ref, b_ref, c_ref, out_ref, False)


def triangle_kernel(a_ref, b_ref, c_ref, out_ref, low):
    n = BLOCK // 2
    row = lax.broadcasted_iota(jnp.int32, (n, n), 0)
    col = lax.broadcasted_iota(jnp.int32, (n, n), 1)
    kept = row >= col if low else row <= col
    halves = (slice(0, n), slice(n, BLOCK))
    one, both = halves if low else halves[::-1]
    for h in range(HEADS):
        cols = slice(h * HEAD_DIM, (h + 1) * HEAD_DIM)

        def part(i, j):
            s = dot(a_ref[i, cols], b_ref[j, cols], ((1,), (1,)))
            if i == j:
                s = jnp.where(kept, s, 0.0)
            return dot(s.astype(BF16), c_ref[j, cols], ((1,), (0,)))

        out_ref[one, cols] = part(one, one)
        out_ref[both, cols] = part(both, one) + part(both, both)


def scan_kernel(core_ref, r_ref, total_ref, pre_ref):
    n = r_ref.shape[0]
    total = r_ref[0]
    for i in range(1, n):
        total = total + r_ref[i]
    total_ref[...] = total
    up = core_ref[0] == 0

    @pl.when(up)
    def _():
        acc = jnp.zeros_like(total)
        for i in range(n):
            pre_ref[i] = acc
            acc = acc + r_ref[i]

    @pl.when(jnp.logical_not(up))
    def _():
        acc = jnp.zeros_like(total)
        for i in reversed(range(n)):
            pre_ref[i] = acc
            acc = acc + r_ref[i]


def final_kernel(
    core_ref, chip_ref, recv_ref, kr_ref, v_ref, o_ref, cos_ref, sin_ref, dq_ref, dk_ref, dv_ref,
    gq_hbm, gk_hbm, gv_hbm, gq_ref, gk_ref, gv_ref, sems, *, scale,
):
    core = core_ref[0]
    copies = []

    def leave(src, dst, cols):
        copy = pltpu.make_async_copy(src.at[:, cols], dst.at[:, cols], sems.at[len(copies)])
        copy.start()
        copies.append(copy)

    cosine = cos_ref[...] * scale
    sine = sin_ref[...] * scale
    for h in range(HEADS):
        cols = slice(h * HEAD_DIM, (h + 1) * HEAD_DIM)
        rows = cols
        chip, recv = chip_ref[rows, :], recv_ref[rows, :]
        prior = jnp.where(core == 0, chip, recv).astype(BF16)
        later = jnp.where(core == 0, recv, chip).astype(BF16)
        dq = dq_ref[:, cols] + dot(o_ref[:, cols], prior, ((1,), (1,)))
        gq_ref[:, cols] = (dq * cosine - pltpu.roll(dq, HALF, 1) * sine).astype(BF16)
        leave(gq_ref, gq_hbm, cols)
        dk = dk_ref[:, cols] + dot(v_ref[:, cols], later, ((1,), (1,)))
        gk_ref[:, cols] = (dk * cosine - pltpu.roll(dk, HALF, 1) * sine).astype(BF16)
        leave(gk_ref, gk_hbm, cols)
        dv = dv_ref[:, cols] + dot(kr_ref[:, cols], later, ((1,), (0,)))
        gv_ref[:, cols] = (dv * scale).astype(BF16)
        leave(gv_ref, gv_hbm, cols)
    for copy in copies:
        copy.wait()


def call(kernel, outs, in_specs, cost, out_spec=WHOLE, scratch=()):
    return pl.pallas_call(
        kernel,
        out_shape=tuple(jax.ShapeDtypeStruct(s, d) for s, d in outs),
        in_specs=in_specs,
        out_specs=tuple(out_spec for _ in outs),
        scratch_shapes=scratch,
        compiler_params=params(),
        cost_estimate=pl.CostEstimate(flops=cost[0], bytes_accessed=cost[1], transcendentals=0),
    )


def shards(queries, keys, values, grad_out, positions):
    ny, nz, nx = lax.axis_size("y"), lax.axis_size("z"), lax.axis_size("x")
    scale = 1.0 / math.sqrt(HEAD_DIM * BLOCK * ny * nz * nx * 2)
    core = lax.axis_index("core")
    core_s = core.astype(jnp.int32)[None]
    wide, state, table = (BLOCK, WIDTH), (WIDTH, HEAD_DIM), (BLOCK, HEAD_DIM)
    groups = BLOCK // HEAD_DIM
    qr, kr, v, o, cosine, sine, mine, other = call(
        rotate_kernel,
        [(wide, BF16)] * 4 + [(table, F32)] * 2 + [(state, F32)] * 2,
        [SCALAR] + [HBM] * 6,
        (2 * 8 * 512 * 128 * 128, 4 << 20),
        scratch=[
            pltpu.VMEM((groups, HEAD_DIM), jnp.int32),
            pltpu.VMEM((1, HEAD_DIM), F32),
            pltpu.VMEM(wide, BF16),
            pltpu.VMEM(wide, BF16),
            pltpu.SemaphoreType.DMA((2,)),
            pltpu.SemaphoreType.DMA((4 * HEADS,)),
        ],
    )(core_s, *[
        pltpu.with_memory_space_constraint(a, pltpu.HBM)
        for a in (positions.reshape(groups, HEAD_DIM), jnp.asarray(FREQUENCY), queries, keys, values, grad_out)
    ])

    def triangle(kernel, a, b, c):
        return call(kernel, [(wide, F32)], [WHOLE] * 3, (2 * 4 * 2 * 512 * 512 * 128, 3 << 20))(a, b, c)[0]

    swap = [(0, 1), (1, 0)]
    chips = nz * nx
    piece = (WIDTH // chips, HEAD_DIM)
    came = lax.ppermute(other, "core", swap)
    dv = triangle(upper_kernel, kr, qr, o)
    came, dv = lax.optimization_barrier((came, dv))
    pieces = lax.all_to_all((mine + came).reshape((chips,) + piece), ("z", "x"), 0, 0)
    total, pre = call(
        scan_kernel, [(piece, F32), ((chips,) + piece, F32)], [SCALAR, WHOLE], (0, 1 << 19)
    )(core_s, pieces)
    y = lax.axis_index("y")
    total, o, v = lax.optimization_barrier((total, o, v))
    others = [lax.ppermute(total, "y", [(i, i ^ step) for i in range(ny)]) for step in (2, 3, 1)]
    dq = triangle(lower_kernel, o, v, kr)
    dk = triangle(upper_kernel, v, o, qr)
    others, dq, dk = lax.optimization_barrier((others, dq, dk))
    above = jnp.zeros(piece, F32)
    for step, came in zip((2, 3, 1), others):
        wanted = jnp.where(core == 0, (y ^ step) < y, (y ^ step) > y)
        above = above + jnp.where(wanted, came, 0.0)
    chip = lax.all_to_all(pre + above[None], ("z", "x"), 0, 0).reshape(state)
    came = lax.ppermute(chip + mine, "core", swap)

    def final(*refs):
        final_kernel(*refs, scale=scale)

    return call(
        final,
        [(wide, BF16)] * 3,
        [SCALAR] + [WHOLE] * 10,
        (2 * 4 * 3 * 512 * 128 * 128, 7 << 20),
        out_spec=HBM,
        scratch=[pltpu.VMEM(wide, BF16)] * 3 + [pltpu.SemaphoreType.DMA((3 * HEADS,))],
    )(core_s, chip, came, kr, v, o, cosine, sine, dq, dk, dv)


def solution(mesh):
    ny = mesh.shape["grp"]
    nz, nx = 8, 4
    fine = Mesh(mesh.devices.reshape(ny, nz, nx, 2), ("y", "z", "x", "core"))
    every = ("y", "z", "x", "core")
    return jax.shard_map(
        shards,
        mesh=fine,
        in_specs=(P(every, None),) * 4 + (P(every),),
        out_specs=(P(every, None),) * 3,
        check_vma=False,
    )
```

time: 65.8 us -> 62.6 us (0.951)
  blocking collectives: 35.7 us -> 14.4 us
  starting transfers between devices: 11.9 us -> 21 us
  waiting for transfers between devices: 4.22 us -> 13.1 us
  local copies, waits for them, and re-layouts: 4.84 us -> 0.71 us
  Pallas kernels: 7.98 us -> 11.5 us
  other arithmetic: 0.1 us -> 0.79 us
    all_to_all x1 -> x0, blocking collectives: 20.7 us -> none  [shards(): pieces = lax.all_to_all(pair.reshape((chips,) + piece), ('z', 'x'), 0, 0)]
    all_to_all x0 -> x1, waiting for transfers between devices: none -> 12 us  [shards(): lax.all_to_all((mine + came).reshape((chips,) + piece), ('z', 'x'), 0, 0)]
    all_to_all x0 -> x1, starting transfers between devices: none -> 9.42 us  [shards(): lax.all_to_all((mine + came).reshape((chips,) + piece), ('z', 'x'), 0, 0)]
    ppermute x4, waiting for transfers between devices: 4.21 us -> 0.01 us  [the longest x3 0.01 us: shards(): lax.ppermute(total, 'y', [(i, i ^ step) for i in range(ny)])]
    unnamed x16 -> x8, local copies, waits for them, and re-layouts: 4.84 us -> 0.71 us
    pallas_call x2 -> x4, Pallas kernels: 5.66 us -> 8.64 us  [the longest x3 5.03 us: triangle(): call(kernel, [(wide, F32)], [WHOLE] * 3, (2 * 4 * 2 * 512 * 512 * 128, 3...]
    ppermute x1, waiting for transfers between devices: 0.01 us -> 1.16 us  [shards(): came = lax.ppermute(chip + mine, 'core', swap)]
    pallas_call x1, Pallas kernels: 0.07 us -> 1.02 us  [shards(): call(scan_kernel, [(piece, F32), ((chips,) + piece, F32)], [SCALAR, WHOLE...]
  transfers between devices with their start and end apart: 5 -> 6, of which waited for: 3 -> 2; matrix products, arithmetic and copies ran while one was open for 0% -> 0% of each run, Pallas kernels for 6% -> 8%
where the time goes in v2:
time: 62.6 us; the launch traced here: 62.3 us
  starting transfers between devices  21 us (34%)
  blocking collectives  14.4 us (23%)
  waiting for transfers between devices  13.1 us (21%)
  Pallas kernels  11.5 us (18%)
  other arithmetic  0.79 us (1%)
  between operations  0.78 us (1%)
  local copies, waits for them, and re-layouts  0.71 us (1%)
    all_to_all x1, blocking collectives, shards(): chip = lax.all_to_all(pre + above[None], ('z', 'x'), 0, 0).reshape(state)  14.4 us
    all_to_all x1, waiting for transfers between devices, shards(): lax.all_to_all((mine + came).reshape((chips,) + piece), ('z', 'x'), 0, 0)  12 us
    all_to_all x1, starting transfers between devices, shards(): lax.all_to_all((mine + came).reshape((chips,) + piece), ('z', 'x'), 0, 0)  9.42 us
    pallas_call x3, Pallas kernels, triangle(): call(kernel, [(wide, F32)], [WHOLE] * 3, (2 * 4 * 2 * 512 * 512 * 128, 3...  5.03 us
    ppermute x1, starting transfers between devices, shards(): came = lax.ppermute(chip + mine, 'core', swap)  4.36 us
    ppermute x3, starting transfers between devices, shards(): lax.ppermute(total, 'y', [(i, i ^ step) for i in range(ny)])  4.01 us
    pallas_call x1, Pallas kernels, shards(): call(rotate_kernel, [(wide, BF16)] * 4 + [(table, F32)] * 2 + [(state, F3...  3.62 us
    ppermute x1, starting transfers between devices, shards(): came = lax.ppermute(other, 'core', swap)  3.24 us
  transfers between devices with their start and end apart: 6, of which 2 were waited for; matrix products, arithmetic and copies ran while one was open for 0% of the time, Pallas kernels for 8%

profile of v2, /device:TPU:1, one launch (start us, length us, event | category | flops | bytes accessed | tf_op | source)
XLA Modules:
  0.0 62.3 jit_solution(6086250552546286331)
XLA Ops:
  0.6 3.6 %shard_map.85 = (bf16[512,512]{1,0:T(8,128)(2,1)S(1)}, bf16[512,512]{1,0:T(8,128)(2,1)S(1)}, bf16[512,512]{1,0:T(8,128)(2,1)S(1)}, bf16[512,512]{1,0:T(8,128)(2,...) custom-call(s32[1]{0:T(128)} %bitcast.core_ref.refs_0_, ...), custom_call_target="tpu_custom_call" | custom-call | flops 134217728 | bytes 4194304 | tf_op jit(solution)/shard_map/pallas_call | solution.py:209
  4.3 0.0 copy-start.2
  4.3 0.7 %copy-done.2 = f32[512,128]{1,0:T(8,128)} copy-done((f32[512,128]{1,0:T(8,128)}, f32[512,128]{1,0:T(8,128)S(1)}, u32[]{:S(2)}) %copy-start.2) | copy-done | bytes 262168
  5.0 0.0 copy-start
  5.0 3.2 %collective-permute-start = (f32[512,128]{1,0:T(8,128)S(1)}, f32[512,128]{1,0:T(8,128)S(1)}, u32[]{:S(2)}, u32[]{:S(2)}) collective-permute-start(f32[512,128]{1,0:T(8,128)S(1)} %get-tuple-element.24), channel_id=1, source_target_pairs={{0,1},{1,0},{2,3},{3,2},{4,5},{5,4},{6,7},{7,6},{8,9},{9,8},{10,11... | collective-permute-start | bytes 786440 | tf_op jit(solution)/shard_map/ppermute | solution.py:233
  8.2 1.7 %shard_map.86.refs_10_ = f32[512,512]{1,0:T(8,128)S(1)} custom-call(bf16[512,512]{1,0:T(8,128)(2,1)S(1)} %get-tuple-element.25.a_ref.c_ref.refs_3_, bf16[512,512]{1,0:T(8,128)(2,1)S(1)} %get-tuple-element.26.b_ref.c_ref, bf16[512,512]{1,0:T(8,128)(2,1)S(1)} %get-tuple-element.33.c_ref.a_ref.b_ref.refs_5_), custom_call_target="tpu_custom_call" | custom-call | flops 536870912 | bytes 3145728 | tf_op jit(solution)/shard_map/pallas_call | solution.py:228
  9.9 0.0 copy-done
  9.9 0.0 collective-permute-done
  9.9 0.7 %add.20 = f32[512,128]{1,0:T(8,128)} add(f32[512,128]{1,0:T(8,128)S(1)} %get-tuple-element.23, f32[512,128]{1,0:T(8,128)S(1)} %collective-permute-done) | non-fusion elementwise | flops 65536 | bytes 786432 | tf_op jit(solution)/shard_map/add | solution.py:236
  10.6 9.4 %all-to-all-start = ((f32[32,16,128]{2,1,0:T(8,128)}), f32[32,16,128]{2,1,0:T(8,128)}, u32[]{:S(2)}, u32[]{:S(2)}) async-start(f32[32,16,128]{2,1,0:T(8,128)} %bitcast.6), calls=%async_computation | async-start | bytes 524288 | tf_op jit(solution)/shard_map/all_to_all | solution.py:236
  20.1 12.0 %all-to-all-done.r_ref = f32[32,16,128]{2,1,0:T(8,128)} async-done(((f32[32,16,128]{2,1,0:T(8,128)}), f32[32,16,128]{2,1,0:T(8,128)}, u32[]{:S(2)}, u32[]{:S(2)}) %all-to-all-start) | async-done | bytes 262176 | tf_op jit(solution)/shard_map/all_to_all | solution.py:236
  32.1 1.0 %shard_map.87 = (f32[16,128]{1,0:T(8,128)S(1)}, f32[32,16,128]{2,1,0:T(8,128)S(1)}) custom-call(s32[1]{0:T(128)} %bitcast.core_ref.refs_0_, f32[32,16,128]{2,1,0:T(8,128)} %all-to-all-done.r_ref), custom_call_target="tpu_custom_call" | custom-call | bytes 524288 | tf_op jit(solution)/shard_map/pallas_call | solution.py:237
  33.1 1.4 %collective-permute-start.3 = (f32[16,128]{1,0:T(8,128)S(1)}, f32[16,128]{1,0:T(8,128)S(1)}, u32[]{:S(2)}, u32[]{:S(2)}) collective-permute-start(f32[16,128]{1,0:T(8,128)S(1)} %get-tuple-element.32), channel_id=1, source_target_pairs={{0,64},{64,0},{128,192},{192,128},{1,65},{65,1},{129,193},{193,129... | collective-permute-start | bytes 24584 | tf_op jit(solution)/shard_map/ppermute | solution.py:242
  34.5 1.9 %collective-permute-start.2 = (f32[16,128]{1,0:T(8,128)S(1)}, f32[16,128]{1,0:T(8,128)S(1)}, u32[]{:S(2)}, u32[]{:S(2)}) collective-permute-start(f32[16,128]{1,0:T(8,128)S(1)} %get-tuple-element.32), channel_id=1, source_target_pairs={{0,192},{64,128},{128,64},{192,0},{1,193},{65,129},{129,65},{193,1... | collective-permute-start | bytes 24584 | tf_op jit(solution)/shard_map/ppermute | solution.py:242
  36.4 0.7 %collective-permute-start.1 = (f32[16,128]{1,0:T(8,128)S(1)}, f32[16,128]{1,0:T(8,128)S(1)}, u32[]{:S(2)}, u32[]{:S(2)}) collective-permute-start(f32[16,128]{1,0:T(8,128)S(1)} %get-tuple-element.32), channel_id=1, source_target_pairs={{0,128},{64,192},{128,0},{192,64},{1,129},{65,193},{129,1},{193,65... | collective-permute-start | bytes 24584 | tf_op jit(solution)/shard_map/ppermute | solution.py:242
  37.1 1.7 %shard_map.89.refs_9_ = f32[512,512]{1,0:T(8,128)S(1)} custom-call(bf16[512,512]{1,0:T(8,128)(2,1)S(1)} %get-tuple-element.34.b_ref.a_ref.refs_4_, bf16[512,512]{1,0:T(8,128)(2,1)S(1)} %get-tuple-element.33.c_ref.a_ref.b_ref.refs_5_, bf16[512,512]{1,0:T(8,128)(2,1)S(1)} %get-tuple-element.26.b_ref.c_ref), custom_call_target="tpu_custom_call" | custom-call | flops 536870912 | bytes 3145728 | tf_op jit(solution)/shard_map/pallas_call | solution.py:228
  38.8 1.7 %shard_map.88.refs_8_ = f32[512,512]{1,0:T(8,128)S(1)} custom-call(bf16[512,512]{1,0:T(8,128)(2,1)S(1)} %get-tuple-element.33.c_ref.a_ref.b_ref.refs_5_, bf16[512,512]{1,0:T(8,128)(2,1)S(1)} %get-tuple-element.34.b_ref.a_ref.refs_4_, bf16[512,512]{1,0:T(8,128)(2,1)S(1)} %get-tuple-element.25.a_ref.c_ref.refs_3_), custom_call_target="tpu_custom_call" | custom-call | flops 536870912 | bytes 3145728 | tf_op jit(solution)/shard_map/pallas_call | solution.py:228
  40.5 0.0 collective-permute-done.3
  40.5 0.0 collective-permute-done.2
  40.5 0.0 collective-permute-done.1
  40.5 14.4 %all_to_all.10 = f32[32,16,128]{2,1,0:T(8,128)S(1)} all-to-all(f32[32,16,128]{2,1,0:T(8,128)S(1)} %broadcast_add_fusion), channel_id=1, replica_groups=mesh['y'=4,'z'=8,'x'=4,'core'=2] {'z','x'}, dimensions={0} | all-to-all | bytes 524288 | tf_op jit(solution)/shard_map/all_to_all | solution.py:250
  54.9 0.0 copy-start.1
  54.9 0.0 copy-start.3
  54.9 4.4 %collective-permute-start.4 = (f32[512,128]{1,0:T(8,128)S(1)}, f32[512,128]{1,0:T(8,128)S(1)}, u32[]{:S(2)}, u32[]{:S(2)}) collective-permute-start(f32[512,128]{1,0:T(8,128)S(1)} %bitcast_add_fusion), channel_id=1, source_target_pairs={{0,1},{1,0},{2,3},{3,2},{4,5},{5,4},{6,7},{7,6},{8,9},{9,8},{10,11... | collective-permute-start | bytes 786440 | tf_op jit(solution)/shard_map/ppermute | solution.py:251
  59.3 1.2 %collective-permute-done.4.refs_2_ = f32[512,128]{1,0:T(8,128)S(1)} collective-permute-done((f32[512,128]{1,0:T(8,128)S(1)}, f32[512,128]{1,0:T(8,128)S(1)}, u32[]{:S(2)}, u32[]{:S(2)}) %collective-permute-start.4) | collective-permute-done | bytes 262176 | tf_op jit(solution)/shard_map/ppermute | solution.py:251
  60.5 0.0 copy-done.1
  60.5 0.0 copy-done.3
  60.5 1.9 %shard_map.90 = (bf16[512,512]{1,0:T(8,128)(2,1)}, bf16[512,512]{1,0:T(8,128)(2,1)}, bf16[512,512]{1,0:T(8,128)(2,1)}) custom-call(s32[1]{0:T(128)} %bitcast.core_ref.refs_0_, f32[512,128]{1,0:T(8,128)S(1)} %bitcast.5, f32[512,128]{1,0:T(8,128)S(1)} %collective-permute-done.4.refs_2_, bf16[512,512]{1,0:T(8,128)(2,1)S(1)} %get-tuple-element.25.a_ref.c_ref.refs_3_, ...), custom_call_target="tpu_custom_call" | custom-call | flops 201326592 | bytes 7340032 | tf_op jit(solution)/shard_map/pallas_call | solution.py:256
  (3 shorter events, 0.1 us)
Async XLA Ops:
  4.3 0.7 %copy-start.2 = (f32[512,128]{1,0:T(8,128)}, f32[512,128]{1,0:T(8,128)S(1)}, u32[]{:S(2)}) copy-start(f32[512,128]{1,0:T(8,128)S(1)} %get-tuple-element.39.refs_7_) | copy-start | bytes 786436
  5.0 4.9 %copy-start = (f32[512,128]{1,0:T(8,128)}, f32[512,128]{1,0:T(8,128)S(1)}, u32[]{:S(2)}) copy-start(f32[512,128]{1,0:T(8,128)S(1)} %get-tuple-element.38.refs_6_) | copy-start | bytes 786436
  5.0 4.9 %collective-permute-start = (f32[512,128]{1,0:T(8,128)S(1)}, f32[512,128]{1,0:T(8,128)S(1)}, u32[]{:S(2)}, u32[]{:S(2)}) collective-permute-start(f32[512,128]{1,0:T(8,128)S(1)} %get-tuple-element.24), channel_id=1, source_target_pairs={{0,1},{1,0},{2,3},{3,2},{4,5},{5,4},{6,7},{7,6},{8,9},{9,8},{10,11... | collective-permute-start | bytes 786440 | tf_op jit(solution)/shard_map/ppermute | solution.py:233
  10.6 21.4 %all-to-all-start = ((f32[32,16,128]{2,1,0:T(8,128)}), f32[32,16,128]{2,1,0:T(8,128)}, u32[]{:S(2)}, u32[]{:S(2)}) async-start(f32[32,16,128]{2,1,0:T(8,128)} %bitcast.6), calls=%async_computation | async-start | bytes 524288 | tf_op jit(solution)/shard_map/all_to_all | solution.py:236
  33.1 7.4 %collective-permute-start.3 = (f32[16,128]{1,0:T(8,128)S(1)}, f32[16,128]{1,0:T(8,128)S(1)}, u32[]{:S(2)}, u32[]{:S(2)}) collective-permute-start(f32[16,128]{1,0:T(8,128)S(1)} %get-tuple-element.32), channel_id=1, source_target_pairs={{0,64},{64,0},{128,192},{192,128},{1,65},{65,1},{129,193},{193,129... | collective-permute-start | bytes 24584 | tf_op jit(solution)/shard_map/ppermute | solution.py:242
  34.5 6.0 %collective-permute-start.2 = (f32[16,128]{1,0:T(8,128)S(1)}, f32[16,128]{1,0:T(8,128)S(1)}, u32[]{:S(2)}, u32[]{:S(2)}) collective-permute-start(f32[16,128]{1,0:T(8,128)S(1)} %get-tuple-element.32), channel_id=1, source_target_pairs={{0,192},{64,128},{128,64},{192,0},{1,193},{65,129},{129,65},{193,1... | collective-permute-start | bytes 24584 | tf_op jit(solution)/shard_map/ppermute | solution.py:242
  36.4 4.1 %collective-permute-start.1 = (f32[16,128]{1,0:T(8,128)S(1)}, f32[16,128]{1,0:T(8,128)S(1)}, u32[]{:S(2)}, u32[]{:S(2)}) collective-permute-start(f32[16,128]{1,0:T(8,128)S(1)} %get-tuple-element.32), channel_id=1, source_target_pairs={{0,128},{64,192},{128,0},{192,64},{1,129},{65,193},{129,1},{193,65... | collective-permute-start | bytes 24584 | tf_op jit(solution)/shard_map/ppermute | solution.py:242
  54.9 5.6 %copy-start.1 = (f32[512,128]{1,0:T(8,128)S(1)}, f32[512,128]{1,0:T(8,128)}, u32[]{:S(2)}) copy-start(f32[512,128]{1,0:T(8,128)} %copy-done) | copy-start | bytes 786436
  54.9 5.6 %copy-start.3 = (f32[512,128]{1,0:T(8,128)S(1)}, f32[512,128]{1,0:T(8,128)}, u32[]{:S(2)}) copy-start(f32[512,128]{1,0:T(8,128)} %copy-done.2) | copy-start | bytes 786436
  54.9 5.5 %collective-permute-start.4 = (f32[512,128]{1,0:T(8,128)S(1)}, f32[512,128]{1,0:T(8,128)S(1)}, u32[]{:S(2)}, u32[]{:S(2)}) collective-permute-start(f32[512,128]{1,0:T(8,128)S(1)} %bitcast_add_fusion), channel_id=1, source_target_pairs={{0,1},{1,0},{2,3},{3,2},{4,5},{5,4},{6,7},{7,6},{8,9},{9,8},{10,11... | collective-permute-start | bytes 786440 | tf_op jit(solution)/shard_map/ppermute | solution.py:251

commit v3 on v2

v3 whole, which is shorter than its diff:
```python
import math

import numpy as np
import jax
import jax.numpy as jnp
from jax import lax
from jax.experimental import pallas as pl
from jax.experimental.pallas import tpu as pltpu
from jax.sharding import Mesh, PartitionSpec as P

HEADS = 4
HEAD_DIM = 128
BLOCK = 512
THETA = 500000.0
WIDTH = HEADS * HEAD_DIM
HALF = HEAD_DIM // 2
F32 = jnp.float32
BF16 = jnp.bfloat16
VMEM_LIMIT = 16 * 1024 * 1024
WHOLE = pl.BlockSpec(memory_space=pltpu.VMEM)
HBM = pl.BlockSpec(memory_space=pltpu.HBM)
SCALAR = pl.BlockSpec(memory_space=pltpu.SMEM)

FREQUENCY = np.tile(
    np.power(THETA, -2.0 * np.arange(HALF) / HEAD_DIM), 2
).astype(np.float32)[None, :]

HALF_PI = (1.5703125, 4.837512969970703125e-4, 7.54978995489188216e-8)


def params():
    return pltpu.CompilerParams(vmem_limit_bytes=VMEM_LIMIT)


def sin_cos(angle):
    turns = jnp.floor(angle * (2.0 / math.pi) + 0.5)
    r = angle - turns * HALF_PI[0]
    r = r - turns * HALF_PI[1]
    r = r - turns * HALF_PI[2]
    r2 = r * r
    s = r + r * r2 * (-1.6666654611e-1 + r2 * (8.3321608736e-3 + r2 * -1.9515295891e-4))
    c = 1.0 + r2 * (-0.5 + r2 * (4.166664568298827e-2 + r2 * (-1.388731625493765e-3 + r2 * 2.443315711809948e-5)))
    quadrant = turns.astype(jnp.int32) & 3
    odd = (quadrant & 1) == 1
    sine = jnp.where(odd, c, s)
    cosine = jnp.where(odd, s, c)
    sine = jnp.where(quadrant >= 2, -sine, sine)
    cosine = jnp.where((quadrant == 1) | (quadrant == 2), -cosine, cosine)
    return sine, cosine


def dot(a, b, dims):
    return lax.dot_general(a, b, (dims, ((), ())), preferred_element_type=F32)


def rotate_kernel(
    where_ref, _, pos_hbm, freq_hbm, q_hbm, k_hbm, v_hbm, o_hbm,
    qr_ref, kr_ref, v_ref, o_ref, cos_ref, sin_ref, mine_ref, other_ref,
    pos_ref, freq_ref, q_ref, k_ref, small_sems, sems,
):
    core = where_ref[0]
    small = [
        pltpu.make_async_copy(pos_hbm, pos_ref, small_sems.at[0]),
        pltpu.make_async_copy(freq_hbm, freq_ref, small_sems.at[1]),
    ]
    for copy in small:
        copy.start()
    copies = []
    for src, dst in ((k_hbm, k_ref), (v_hbm, v_ref), (q_hbm, q_ref), (o_hbm, o_ref)):
        of_array = [
            pltpu.make_async_copy(src.at[rows, :], dst.at[rows, :], sems.at[len(copies) * 1 + i])
            for i, rows in enumerate(slice(r * 512, (r + 1) * 512) for r in range(1))
        ]
        copies.append(of_array)
    for copy in copies[0] + copies[1]:
        copy.start()
    first = lax.broadcasted_iota(jnp.int32, (HEAD_DIM, HEAD_DIM), 1) < HALF
    for copy in small:
        copy.wait()
    for copy in copies[2] + copies[3]:
        copy.start()
    for i in range(BLOCK // HEAD_DIM):
        row = jnp.broadcast_to(pos_ref[i : i + 1, :].astype(F32), (HEAD_DIM, HEAD_DIM))
        sine, cosine = sin_cos(row.T * freq_ref[...])
        rows = slice(i * HEAD_DIM, (i + 1) * HEAD_DIM)
        cos_ref[rows, :] = cosine
        sin_ref[rows, :] = jnp.where(first, -sine, sine)
    def rotated(ref, out_ref, other_ref):
        states = []
        for h in range(HEADS):
            cols = slice(h * HEAD_DIM, (h + 1) * HEAD_DIM)
            a = ref[:, cols].astype(F32)
            rot = (a * cos_ref[...] + pltpu.roll(a, HALF, 1) * sin_ref[...]).astype(BF16)
            out_ref[:, cols] = rot
            states.append(dot(other_ref[:, cols], rot, ((0,), (0,))))
        return states

    for copy in copies[0] + copies[1]:
        copy.wait()
    key_states = rotated(k_ref, kr_ref, v_ref)
    for h in range(HEADS):
        rows = slice(h * HEAD_DIM, (h + 1) * HEAD_DIM)
        mine_ref[rows, :] = key_states[h]
        other_ref[rows, :] = key_states[h]
    for copy in copies[2] + copies[3]:
        copy.wait()
    query_states = rotated(q_ref, qr_ref, o_ref)
    for h in range(HEADS):
        rows = slice(h * HEAD_DIM, (h + 1) * HEAD_DIM)
        mine_ref[rows, :] = jnp.where(core == 0, mine_ref[rows, :], query_states[h])
        other_ref[rows, :] = jnp.where(core == 0, query_states[h], other_ref[rows, :])


def triangle(a_ref, b_ref, c_ref, h, low):
    n = BLOCK // 2
    row = lax.broadcasted_iota(jnp.int32, (n, n), 0)
    col = lax.broadcasted_iota(jnp.int32, (n, n), 1)
    kept = row >= col if low else row <= col
    cols = slice(h * HEAD_DIM, (h + 1) * HEAD_DIM)
    halves = (slice(0, n), slice(n, BLOCK))

    def part(i, j):
        s = dot(a_ref[halves[i], cols], b_ref[halves[j], cols], ((1,), (1,)))
        if i == j:
            s = jnp.where(kept, s, 0.0)
        return dot(s.astype(BF16), c_ref[halves[j], cols], ((1,), (0,)))

    if low:
        return part(0, 0), part(1, 0) + part(1, 1)
    return part(0, 0) + part(0, 1), part(1, 1)


BESIDE_FIRST = (("dv", 0), ("dv", 1), ("dv", 2))
BESIDE_GROUPS = (("dq", 0), ("dq", 1), ("dq", 2), ("dq", 3), ("dk", 0), ("dk", 1))
BESIDE_LAST = (("dk", 2), ("dk", 3), ("dv", 3))
Y_STEPS = (1, 3, 2)


def intra_kernel(qr_ref, kr_ref, v_ref, o_ref, out_ref, *, jobs):
    n = BLOCK // 2
    for i, (kind, h) in enumerate(jobs):
        cols = slice(i * HEAD_DIM, (i + 1) * HEAD_DIM)
        if kind == "dq":
            top, low = triangle(o_ref, v_ref, kr_ref, h, True)
        elif kind == "dk":
            top, low = triangle(v_ref, o_ref, qr_ref, h, False)
        else:
            top, low = triangle(kr_ref, qr_ref, o_ref, h, False)
        out_ref[:n, cols] = top
        out_ref[n:, cols] = low


def scan_kernel(where_ref, r_ref, total_ref, pre_ref):
    n = r_ref.shape[0]
    total = r_ref[0]
    for i in range(1, n):
        total = total + r_ref[i]
    total_ref[...] = total
    up = where_ref[0] == 0

    @pl.when(up)
    def _():
        acc = jnp.zeros_like(total)
        for i in range(n):
            pre_ref[i] = acc
            acc = acc + r_ref[i]

    @pl.when(jnp.logical_not(up))
    def _():
        acc = jnp.zeros_like(total)
        for i in reversed(range(n)):
            pre_ref[i] = acc
            acc = acc + r_ref[i]


def pair_kernel(mine_ref, came_ref, _, out_ref):
    out_ref[...] = mine_ref[...] + came_ref[...]


def place_kernel(where_ref, group_ref, pre_ref, a_ref, b_ref, c_ref, _, out_ref):
    above = jnp.zeros(a_ref.shape, F32)
    up, y = where_ref[0] == 0, group_ref[0]
    for step, ref in zip(Y_STEPS, (a_ref, b_ref, c_ref)):
        below = (y ^ step) < y
        above = above + jnp.where(up == below, ref[...], 0.0)
    out_ref[...] = pre_ref[...] + above[None]


def final_kernel(
    where_ref, chip_ref, recv_ref, kr_ref, v_ref, o_ref, cos_ref, sin_ref, first_ref, groups_ref, last_ref,
    gq_hbm, gk_hbm, gv_hbm, gq_ref, gk_ref, gv_ref, sems, *, scale,
):
    core = where_ref[0]
    copies = []

    def intra(kind, h):
        for ref, jobs in ((first_ref, BESIDE_FIRST), (groups_ref, BESIDE_GROUPS), (last_ref, BESIDE_LAST)):
            if (kind, h) in jobs:
                i = jobs.index((kind, h))
                return ref[:, i * HEAD_DIM : (i + 1) * HEAD_DIM]

    def leave(src, dst, cols):
        copy = pltpu.make_async_copy(src.at[:, cols], dst.at[:, cols], sems.at[len(copies)])
        copy.start()
        copies.append(copy)

    cosine = cos_ref[...] * scale
    sine = sin_ref[...] * scale
    for h in range(HEADS):
        cols = slice(h * HEAD_DIM, (h + 1) * HEAD_DIM)
        rows = cols
        chip, recv = chip_ref[rows, :], recv_ref[rows, :]
        prior = jnp.where(core == 0, chip, recv).astype(BF16)
        later = jnp.where(core == 0, recv, chip).astype(BF16)
        dq = intra("dq", h) + dot(o_ref[:, cols], prior, ((1,), (0,)))
        gq_ref[:, cols] = (dq * cosine - pltpu.roll(dq, HALF, 1) * sine).astype(BF16)
        leave(gq_ref, gq_hbm, cols)
        dk = intra("dk", h) + dot(v_ref[:, cols], later, ((1,), (0,)))
        gk_ref[:, cols] = (dk * cosine - pltpu.roll(dk, HALF, 1) * sine).astype(BF16)
        leave(gk_ref, gk_hbm, cols)
        dv = intra("dv", h) + dot(kr_ref[:, cols], later, ((1,), (1,)))
        gv_ref[:, cols] = (dv * scale).astype(BF16)
        leave(gv_ref, gv_hbm, cols)
    for copy in copies:
        copy.wait()


def call(kernel, outs, in_specs, cost, out_spec=WHOLE, scratch=()):
    return pl.pallas_call(
        kernel,
        out_shape=tuple(jax.ShapeDtypeStruct(s, d) for s, d in outs),
        in_specs=in_specs,
        out_specs=tuple(out_spec for _ in outs),
        scratch_shapes=scratch,
        compiler_params=params(),
        cost_estimate=pl.CostEstimate(flops=cost[0], bytes_accessed=cost[1], transcendentals=0),
    )


def shards(queries, keys, values, grad_out, positions):
    ny, nz, nx = lax.axis_size("y"), lax.axis_size("z"), lax.axis_size("x")
    scale = 1.0 / math.sqrt(HEAD_DIM * BLOCK * ny * nz * nx * 2)
    where = lax.axis_index("core").astype(jnp.int32)[None]
    group = lax.axis_index("y").astype(jnp.int32)[None]
    wide, state, table = (BLOCK, WIDTH), (WIDTH, HEAD_DIM), (BLOCK, HEAD_DIM)
    groups = BLOCK // HEAD_DIM
    qr, kr, v, o, cosine, sine, mine, other = call(
        rotate_kernel,
        [(wide, BF16)] * 4 + [(table, F32)] * 2 + [(state, F32)] * 2,
        [SCALAR] * 2 + [HBM] * 6,
        (2 * 8 * 512 * 128 * 128, 4 << 20),
        scratch=[
            pltpu.VMEM((groups, HEAD_DIM), jnp.int32),
            pltpu.VMEM((1, HEAD_DIM), F32),
            pltpu.VMEM(wide, BF16),
            pltpu.VMEM(wide, BF16),
            pltpu.SemaphoreType.DMA((2,)),
            pltpu.SemaphoreType.DMA((4 * HEADS,)),
        ],
    )(where, group, *[
        pltpu.with_memory_space_constraint(a, pltpu.HBM)
        for a in (positions.reshape(groups, HEAD_DIM), jnp.asarray(FREQUENCY), queries, keys, values, grad_out)
    ])

    def intra(jobs, after=()):
        def kernel(*refs):
            intra_kernel(*refs[:4], refs[-1], jobs=jobs)

        shape = (BLOCK, len(jobs) * HEAD_DIM)
        work = 2 * len(jobs) * 2 * BLOCK * BLOCK * HEAD_DIM
        specs = [WHOLE] * (4 + len(after))
        return call(kernel, [(shape, F32)], specs, (work, 3 << 20))(qr, kr, v, o, *after)[0]

    swap = [(0, 1), (1, 0)]
    chips = nz * nx
    piece = (WIDTH // chips, HEAD_DIM)
    came = lax.ppermute(other, "core", swap)
    first = intra(BESIDE_FIRST)
    (pair,) = call(pair_kernel, [(state, F32)], [WHOLE] * 3, (0, 1 << 19))(mine, came, first)
    pieces = lax.all_to_all(pair.reshape((chips,) + piece), ("z", "x"), 0, 0)
    total, pre = call(
        scan_kernel, [(piece, F32), ((chips,) + piece, F32)], [SCALAR, WHOLE], (0, 1 << 19)
    )(where, pieces)
    groups = intra(BESIDE_GROUPS, (total,))
    others = [lax.ppermute(total, "y", [(i, i ^ step) for i in range(ny)]) for step in Y_STEPS]
    (place,) = call(
        place_kernel, [((chips,) + piece, F32)], [SCALAR] * 2 + [WHOLE] * 5, (0, 1 << 19)
    )(where, group, pre, *others, groups)
    chip = lax.all_to_all(place, ("z", "x"), 0, 0).reshape(state)
    last = intra(BESIDE_LAST, (chip,))
    came = lax.ppermute(chip + mine, "core", swap)

    def final(*refs):
        final_kernel(*refs, scale=scale)

    return call(
        final,
        [(wide, BF16)] * 3,
        [SCALAR] + [WHOLE] * 10,
        (2 * 4 * 3 * 512 * 128 * 128, 7 << 20),
        out_spec=HBM,
        scratch=[pltpu.VMEM(wide, BF16)] * 3 + [pltpu.SemaphoreType.DMA((3 * HEADS,))],
    )(where, chip, came, kr, v, o, cosine, sine, first, groups, last)


def solution(mesh):
    ny = mesh.shape["grp"]
    nz, nx = 8, 4
    fine = Mesh(mesh.devices.reshape(ny, nz, nx, 2), ("y", "z", "x", "core"))
    every = ("y", "z", "x", "core")
    return jax.shard_map(
        shards,
        mesh=fine,
        in_specs=(P(every, None),) * 4 + (P(every),),
        out_specs=(P(every, None),) * 3,
        check_vma=False,
    )
```

time: 62.6 us -> 58.3 us (0.931)
  blocking collectives: 14.4 us -> 35.2 us
  waiting for transfers between devices: 13.1 us -> 0.85 us
  starting transfers between devices: 21 us -> 11.3 us
  Pallas kernels: 11.5 us -> 9.96 us
  other arithmetic: 0.79 us -> 0.04 us
  local copies, waits for them, and re-layouts: 0.71 us -> 0 us
    all_to_all x1 -> x2, blocking collectives: 14.4 us -> 35.2 us  [the longest x1 20.9 us: shards(): pieces = lax.all_to_all(pair.reshape((chips,) + piece), ('z', 'x'), 0, 0)]
    all_to_all x1 -> x0, waiting for transfers between devices: 12 us -> none  [shards(): lax.all_to_all((mine + came).reshape((chips,) + piece), ('z', 'x'), 0, 0)]
    all_to_all x1 -> x0, starting transfers between devices: 9.42 us -> none  [shards(): lax.all_to_all((mine + came).reshape((chips,) + piece), ('z', 'x'), 0, 0)]
    ppermute x1, waiting for transfers between devices: 1.16 us -> 0.01 us  [shards(): came = lax.ppermute(chip + mine, 'core', swap)]
    pallas_call x1, Pallas kernels: 1.02 us -> 0.07 us  [shards(): call(scan_kernel, [(piece, F32), ((chips,) + piece, F32)], [SCALAR, WHOLE...]
    ppermute x3, waiting for transfers between devices: 0.01 us -> 0.85 us  [shards(): lax.ppermute(total, 'y', [(i, i ^ step) for i in range(ny)])]
    pallas_call x1, Pallas kernels: 3.62 us -> 2.85 us  [shards(): call(rotate_kernel, [(wide, BF16)] * 4 + [(table, F32)] * 2 + [(state, F3...]
    add x3 -> x0, other arithmetic: 0.76 us -> none  [the longest x1 0.73 us: shards(): mine + came]
  transfers between devices with their start and end apart: 6 -> 5, of which waited for: 2 -> 1; matrix products, arithmetic and copies ran while one was open for 0% -> 0% of each run, Pallas kernels for 8% -> 9%
where the time goes in v3:
time: 58.3 us; the launch traced here: 58.1 us
  blocking collectives  35.2 us (60%)
  starting transfers between devices  11.3 us (19%)
  Pallas kernels  9.96 us (17%)
  waiting for transfers between devices  0.85 us (1%)
  between operations  0.71 us (1%)
    all_to_all x1, blocking collectives, shards(): pieces = lax.all_to_all(pair.reshape((chips,) + piece), ('z', 'x'), 0, 0)  20.9 us
    all_to_all x1, blocking collectives, shards(): chip = lax.all_to_all(place, ('z', 'x'), 0, 0).reshape(state)  14.3 us
    pallas_call x3, Pallas kernels, intra(): call(kernel, [(shape, F32)], specs, (work, 3 << 20))(qr, kr, v, o, *after)  5.03 us
    ppermute x1, starting transfers between devices, shards(): came = lax.ppermute(chip + mine, 'core', swap)  4.2 us
    ppermute x3, starting transfers between devices, shards(): lax.ppermute(total, 'y', [(i, i ^ step) for i in range(ny)])  3.78 us
    ppermute x1, starting transfers between devices, shards(): came = lax.ppermute(other, 'core', swap)  3.33 us
    pallas_call x1, Pallas kernels, shards(): call(rotate_kernel, [(wide, BF16)] * 4 + [(table, F32)] * 2 + [(state, F3...  2.85 us
    pallas_call x1, Pallas kernels, shards(): call(final, [(wide, BF16)] * 3, [SCALAR] + [WHOLE] * 10, (2 * 4 * 3 * 512...  1.95 us
  transfers between devices with their start and end apart: 5, of which 1 were waited for; matrix products, arithmetic and copies ran while one was open for 0% of the time, Pallas kernels for 9%

profile of v3, /device:TPU:1, one launch (start us, length us, event | category | flops | bytes accessed | tf_op | source)
XLA Modules:
  0.0 58.1 jit_solution(9896409296807210045)
XLA Ops:
  0.6 2.9 %shard_map.85 = (bf16[512,512]{1,0:T(8,128)(2,1)S(1)}, bf16[512,512]{1,0:T(8,128)(2,1)S(1)}, bf16[512,512]{1,0:T(8,128)(2,1)S(1)}, bf16[512,512]{1,0:T(8,128)(2,...) custom-call(s32[1]{0:T(128)} %bitcast.where_ref.refs_0_, ...), custom_call_target="tpu_custom_call" | custom-call | flops 134217728 | bytes 4194304 | tf_op jit(solution)/shard_map/pallas_call | solution.py:247
  3.5 3.3 %collective-permute-start = (f32[512,128]{1,0:T(8,128)S(1)}, f32[512,128]{1,0:T(8,128)S(1)}, u32[]{:S(2)}, u32[]{:S(2)}) collective-permute-start(f32[512,128]{1,0:T(8,128)S(1)} %get-tuple-element.14), channel_id=1, source_target_pairs={{0,1},{1,0},{2,3},{3,2},{4,5},{5,4},{6,7},{7,6},{8,9},{9,8},{10,11... | collective-permute-start | bytes 786440 | tf_op jit(solution)/shard_map/ppermute | solution.py:277
  6.8 1.3 %shard_map.86._.refs_8_ = f32[512,384]{1,0:T(8,128)S(1)} custom-call(bf16[512,512]{1,0:T(8,128)(2,1)S(1)} %get-tuple-element.15.refs_0_, bf16[512,512]{1,0:T(8,128)(2,1)S(1)} %get-tuple-element.16.refs_1_.refs_3_, bf16[512,512]{1,0:T(8,128)(2,1)S(1)} %get-tuple-element.17.refs_2_.refs_4_, bf16[512,512]{1,0:T(8,128)(2,1)S(1)} %get-tuple-element.18.refs_3_.refs_5_), custom_call_target="tpu_custom_call" | custom-call | flops 402653184 | bytes 3145728 | tf_op jit(solution)/shard_map/pallas_call | solution.py:272
  8.2 0.0 collective-permute-done.came_ref
  8.2 20.9 %all_to_all.10.r_ref = f32[32,16,128]{2,1,0:T(8,128)S(1)} all-to-all(f32[32,16,128]{2,1,0:T(8,128)S(1)} %bitcast.8), channel_id=1, replica_groups=mesh['y'=4,'z'=8,'x'=4,'core'=2] {'z','x'}, dimensions={0} | all-to-all | bytes 524288 | tf_op jit(solution)/shard_map/all_to_all | solution.py:280
  29.1 0.1 shard_map.88
  29.2 3.0 %collective-permute-start.3 = (f32[16,128]{1,0:T(8,128)S(1)}, f32[16,128]{1,0:T(8,128)S(1)}, u32[]{:S(2)}, u32[]{:S(2)}) collective-permute-start(f32[16,128]{1,0:T(8,128)S(1)} %get-tuple-element.20.refs_4_), channel_id=1, source_target_pairs={{0,128},{64,192},{128,0},{192,64},{1,129},{65,193},{129,1},{193,65... | collective-permute-start | bytes 24584 | tf_op jit(solution)/shard_map/ppermute | solution.py:285
  32.2 0.8 %collective-permute-start.2 = (f32[16,128]{1,0:T(8,128)S(1)}, f32[16,128]{1,0:T(8,128)S(1)}, u32[]{:S(2)}, u32[]{:S(2)}) collective-permute-start(f32[16,128]{1,0:T(8,128)S(1)} %get-tuple-element.20.refs_4_), channel_id=1, source_target_pairs={{0,192},{64,128},{128,64},{192,0},{1,193},{65,129},{129,65},{193,1... | collective-permute-start | bytes 24584 | tf_op jit(solution)/shard_map/ppermute | solution.py:285
  33.0 0.0 collective-permute-start.1
  33.0 2.4 %shard_map.89._.refs_9_ = f32[512,768]{1,0:T(8,128)S(1)} custom-call(bf16[512,512]{1,0:T(8,128)(2,1)S(1)} %get-tuple-element.15.refs_0_, bf16[512,512]{1,0:T(8,128)(2,1)S(1)} %get-tuple-element.16.refs_1_.refs_3_, bf16[512,512]{1,0:T(8,128)(2,1)S(1)} %get-tuple-element.17.refs_2_.refs_4_, bf16[512,512]{1,0:T(8,128)(2,1)S(1)} %get-tuple-element.18.refs_3_.refs_5_, ...), custom_call_target="tpu_custom_call" | custom-call | flops 805306368 | bytes 3145728 | tf_op jit(solution)/shard_map/pallas_call | solution.py:272
  35.4 0.0 collective-permute-done.3.c_ref
  35.4 0.8 %collective-permute-done.2.b_ref = f32[16,128]{1,0:T(8,128)S(1)} collective-permute-done((f32[16,128]{1,0:T(8,128)S(1)}, f32[16,128]{1,0:T(8,128)S(1)}, u32[]{:S(2)}, u32[]{:S(2)}) %collective-permute-start.2) | collective-permute-done | bytes 8224 | tf_op jit(solution)/shard_map/ppermute | solution.py:285
  36.2 0.0 collective-permute-done.1.a_ref
  36.2 14.3 %all_to_all.11 = f32[32,16,128]{2,1,0:T(8,128)S(1)} all-to-all(f32[32,16,128]{2,1,0:T(8,128)S(1)} %shard_map.90), channel_id=1, replica_groups=mesh['y'=4,'z'=8,'x'=4,'core'=2] {'z','x'}, dimensions={0} | all-to-all | bytes 524288 | tf_op jit(solution)/shard_map/all_to_all | solution.py:289
  50.6 4.2 %collective-permute-start.4 = (f32[512,128]{1,0:T(8,128)S(1)}, f32[512,128]{1,0:T(8,128)S(1)}, u32[]{:S(2)}, u32[]{:S(2)}) collective-permute-start(f32[512,128]{1,0:T(8,128)S(1)} %bitcast_add_fusion), channel_id=1, source_target_pairs={{0,1},{1,0},{2,3},{3,2},{4,5},{5,4},{6,7},{7,6},{8,9},{9,8},{10,11... | collective-permute-start | bytes 786440 | tf_op jit(solution)/shard_map/ppermute | solution.py:291
  54.8 1.3 %shard_map.91.refs_10_ = f32[512,384]{1,0:T(8,128)S(1)} custom-call(bf16[512,512]{1,0:T(8,128)(2,1)S(1)} %get-tuple-element.15.refs_0_, bf16[512,512]{1,0:T(8,128)(2,1)S(1)} %get-tuple-element.16.refs_1_.refs_3_, bf16[512,512]{1,0:T(8,128)(2,1)S(1)} %get-tuple-element.17.refs_2_.refs_4_, bf16[512,512]{1,0:T(8,128)(2,1)S(1)} %get-tuple-element.18.refs_3_.refs_5_, ...), custom_call_target="tpu_custom_call" | custom-call | flops 402653184 | bytes 3145728 | tf_op jit(solution)/shard_map/pallas_call | solution.py:272
  56.1 0.0 collective-permute-done.4.refs_2_
  56.1 1.9 %shard_map.92 = (bf16[512,512]{1,0:T(8,128)(2,1)}, bf16[512,512]{1,0:T(8,128)(2,1)}, bf16[512,512]{1,0:T(8,128)(2,1)}) custom-call(s32[1]{0:T(128)} %bitcast.where_ref.refs_0_, f32[512,128]{1,0:T(8,128)S(1)} %bitcast.7, f32[512,128]{1,0:T(8,128)S(1)} %collective-permute-done.4.refs_2_, bf16[512,512]{1,0:T(8,128)(2,1)S(1)} %get-tuple-element.16.refs_1_.refs_3_, ...), custom_call_target="tpu_custom_call" | custom-call | flops 201326592 | bytes 7340032 | tf_op jit(solution)/shard_map/pallas_call | solution.py:296
  (3 shorter events, 0.1 us)
Async XLA Ops:
  3.5 4.7 %collective-permute-start = (f32[512,128]{1,0:T(8,128)S(1)}, f32[512,128]{1,0:T(8,128)S(1)}, u32[]{:S(2)}, u32[]{:S(2)}) collective-permute-start(f32[512,128]{1,0:T(8,128)S(1)} %get-tuple-element.14), channel_id=1, source_target_pairs={{0,1},{1,0},{2,3},{3,2},{4,5},{5,4},{6,7},{7,6},{8,9},{9,8},{10,11... | collective-permute-start | bytes 786440 | tf_op jit(solution)/shard_map/ppermute | solution.py:277
  29.2 6.2 %collective-permute-start.3 = (f32[16,128]{1,0:T(8,128)S(1)}, f32[16,128]{1,0:T(8,128)S(1)}, u32[]{:S(2)}, u32[]{:S(2)}) collective-permute-start(f32[16,128]{1,0:T(8,128)S(1)} %get-tuple-element.20.refs_4_), channel_id=1, source_target_pairs={{0,128},{64,192},{128,0},{192,64},{1,129},{65,193},{129,1},{193,65... | collective-permute-start | bytes 24584 | tf_op jit(solution)/shard_map/ppermute | solution.py:285
  32.2 4.0 %collective-permute-start.2 = (f32[16,128]{1,0:T(8,128)S(1)}, f32[16,128]{1,0:T(8,128)S(1)}, u32[]{:S(2)}, u32[]{:S(2)}) collective-permute-start(f32[16,128]{1,0:T(8,128)S(1)} %get-tuple-element.20.refs_4_), channel_id=1, source_target_pairs={{0,192},{64,128},{128,64},{192,0},{1,193},{65,129},{129,65},{193,1... | collective-permute-start | bytes 24584 | tf_op jit(solution)/shard_map/ppermute | solution.py:285
  33.0 3.2 %collective-permute-start.1 = (f32[16,128]{1,0:T(8,128)S(1)}, f32[16,128]{1,0:T(8,128)S(1)}, u32[]{:S(2)}, u32[]{:S(2)}) collective-permute-start(f32[16,128]{1,0:T(8,128)S(1)} %get-tuple-element.20.refs_4_), channel_id=1, source_target_pairs={{0,64},{64,0},{128,192},{192,128},{1,65},{65,1},{129,193},{193,129... | collective-permute-start | bytes 24584 | tf_op jit(solution)/shard_map/ppermute | solution.py:285
  50.6 5.5 %collective-permute-start.4 = (f32[512,128]{1,0:T(8,128)S(1)}, f32[512,128]{1,0:T(8,128)S(1)}, u32[]{:S(2)}, u32[]{:S(2)}) collective-permute-start(f32[512,128]{1,0:T(8,128)S(1)} %bitcast_add_fusion), channel_id=1, source_target_pairs={{0,1},{1,0},{2,3},{3,2},{4,5},{5,4},{6,7},{7,6},{8,9},{9,8},{10,11... | collective-permute-start | bytes 786440 | tf_op jit(solution)/shard_map/ppermute | solution.py:291

commit v4 on v3

v4 whole, which is shorter than its diff:
```python
import math

import numpy as np
import jax
import jax.numpy as jnp
from jax import lax
from jax.experimental import pallas as pl
from jax.experimental.pallas import tpu as pltpu
from jax.sharding import PartitionSpec as P

HEADS = 4
HEAD_DIM = 128
BLOCK = 512
THETA = 500000.0
WIDTH = HEADS * HEAD_DIM
HALF = HEAD_DIM // 2
F32 = jnp.float32
BF16 = jnp.bfloat16
VMEM_LIMIT = 16 * 1024 * 1024
WHOLE = pl.BlockSpec(memory_space=pltpu.VMEM)
HBM = pl.BlockSpec(memory_space=pltpu.HBM)

FREQUENCY = np.tile(
    np.power(THETA, -2.0 * np.arange(HALF) / HEAD_DIM), 2
).astype(np.float32)[None, :]

HALF_PI = (1.5703125, 4.837512969970703125e-4, 7.54978995489188216e-8)


def params():
    return pltpu.CompilerParams(vmem_limit_bytes=VMEM_LIMIT)


def sin_cos(angle):
    turns = jnp.floor(angle * (2.0 / math.pi) + 0.5)
    r = angle - turns * HALF_PI[0]
    r = r - turns * HALF_PI[1]
    r = r - turns * HALF_PI[2]
    r2 = r * r
    s = r + r * r2 * (-1.6666654611e-1 + r2 * (8.3321608736e-3 + r2 * -1.9515295891e-4))
    c = 1.0 + r2 * (-0.5 + r2 * (4.166664568298827e-2 + r2 * (-1.388731625493765e-3 + r2 * 2.443315711809948e-5)))
    quadrant = turns.astype(jnp.int32) & 3
    odd = (quadrant & 1) == 1
    sine = jnp.where(odd, c, s)
    cosine = jnp.where(odd, s, c)
    sine = jnp.where(quadrant >= 2, -sine, sine)
    cosine = jnp.where((quadrant == 1) | (quadrant == 2), -cosine, cosine)
    return sine, cosine


def dot(a, b, dims):
    return lax.dot_general(a, b, (dims, ((), ())), preferred_element_type=F32)


def rotate_kernel(
    pos_hbm, freq_hbm, q_hbm, k_hbm, v_hbm, o_hbm,
    qr_ref, kr_ref, v_ref, o_ref, cos_ref, sin_ref, mine_ref, other_ref,
    pos_ref, freq_ref, q_ref, k_ref, small_sems, sems,
):
    core = (lax.axis_index("stretch") & 1)
    small = [
        pltpu.make_async_copy(pos_hbm, pos_ref, small_sems.at[0]),
        pltpu.make_async_copy(freq_hbm, freq_ref, small_sems.at[1]),
    ]
    for copy in small:
        copy.start()
    pairs = ((k_hbm, k_ref), (v_hbm, v_ref), (q_hbm, q_ref), (o_hbm, o_ref))
    copies = [pltpu.make_async_copy(src, dst, sems.at[i]) for i, (src, dst) in enumerate(pairs)]
    for copy in copies[:2]:
        copy.start()
    first = lax.broadcasted_iota(jnp.int32, (HEAD_DIM, HEAD_DIM), 1) < HALF
    for copy in small:
        copy.wait()
    for copy in copies[2:]:
        copy.start()
    for i in range(BLOCK // HEAD_DIM):
        row = jnp.broadcast_to(pos_ref[i : i + 1, :].astype(F32), (HEAD_DIM, HEAD_DIM))
        sine, cosine = sin_cos(row.T * freq_ref[...])
        rows = slice(i * HEAD_DIM, (i + 1) * HEAD_DIM)
        cos_ref[rows, :] = cosine
        sin_ref[rows, :] = jnp.where(first, -sine, sine)

    def rotated(ref, out_ref, other_ref):
        states = []
        for h in range(HEADS):
            cols = slice(h * HEAD_DIM, (h + 1) * HEAD_DIM)
            a = ref[:, cols].astype(F32)
            rot = (a * cos_ref[...] + pltpu.roll(a, HALF, 1) * sin_ref[...]).astype(BF16)
            out_ref[:, cols] = rot
            states.append(dot(other_ref[:, cols], rot, ((0,), (0,))))
        return states

    for copy in copies[:2]:
        copy.wait()
    key_states = rotated(k_ref, kr_ref, v_ref)
    for h in range(HEADS):
        rows = slice(h * HEAD_DIM, (h + 1) * HEAD_DIM)
        mine_ref[rows, :] = key_states[h]
        other_ref[rows, :] = key_states[h]
    for copy in copies[2:]:
        copy.wait()
    query_states = rotated(q_ref, qr_ref, o_ref)
    for h in range(HEADS):
        rows = slice(h * HEAD_DIM, (h + 1) * HEAD_DIM)
        mine_ref[rows, :] = jnp.where(core == 0, mine_ref[rows, :], query_states[h])
        other_ref[rows, :] = jnp.where(core == 0, query_states[h], other_ref[rows, :])


def triangle(a_ref, b_ref, c_ref, h, low):
    n = BLOCK // 2
    row = lax.broadcasted_iota(jnp.int32, (n, n), 0)
    col = lax.broadcasted_iota(jnp.int32, (n, n), 1)
    kept = row >= col if low else row <= col
    cols = slice(h * HEAD_DIM, (h + 1) * HEAD_DIM)
    halves = (slice(0, n), slice(n, BLOCK))

    def part(i, j):
        s = dot(a_ref[halves[i], cols], b_ref[halves[j], cols], ((1,), (1,)))
        if i == j:
            s = jnp.where(kept, s, 0.0)
        return dot(s.astype(BF16), c_ref[halves[j], cols], ((1,), (0,)))

    if low:
        return part(0, 0), part(1, 0) + part(1, 1)
    return part(0, 0) + part(0, 1), part(1, 1)


BESIDE_FIRST = (("dv", 0), ("dv", 1), ("dv", 2))
BESIDE_GROUPS = tuple(("dq", h) for h in range(HEADS)) + tuple(("dk", h) for h in range(HEADS)) + (("dv", 3),)
Y_STEPS = (1, 3, 2)


def intra_kernel(qr_ref, kr_ref, v_ref, o_ref, out_ref, *, jobs):
    n = BLOCK // 2
    for i, (kind, h) in enumerate(jobs):
        cols = slice(i * HEAD_DIM, (i + 1) * HEAD_DIM)
        if kind == "dq":
            top, low = triangle(o_ref, v_ref, kr_ref, h, True)
        elif kind == "dk":
            top, low = triangle(v_ref, o_ref, qr_ref, h, False)
        else:
            top, low = triangle(kr_ref, qr_ref, o_ref, h, False)
        out_ref[:n, cols] = top
        out_ref[n:, cols] = low


def scan_kernel(r_ref, total_ref, pre_ref):
    n = r_ref.shape[0]
    token_order = sorted(range(n), key=lambda i: ORDER[i])
    total = r_ref[0]
    for i in range(1, n):
        total = total + r_ref[i]
    total_ref[...] = total
    up = (lax.axis_index("stretch") & 1) == 0

    @pl.when(up)
    def _():
        acc = jnp.zeros_like(total)
        for i in token_order:
            pre_ref[i] = acc
            acc = acc + r_ref[i]

    @pl.when(jnp.logical_not(up))
    def _():
        acc = jnp.zeros_like(total)
        for i in reversed(token_order):
            pre_ref[i] = acc
            acc = acc + r_ref[i]


def pair_kernel(mine_ref, came_ref, _, out_ref):
    out_ref[...] = mine_ref[...] + came_ref[...]


def place_kernel(pre_ref, a_ref, b_ref, c_ref, _, out_ref):
    above = jnp.zeros(a_ref.shape, F32)
    up, y = (lax.axis_index("stretch") & 1) == 0, lax.axis_index("grp")
    for step, ref in zip(Y_STEPS, (a_ref, b_ref, c_ref)):
        below = (y ^ step) < y
        above = above + jnp.where(up == below, ref[...], 0.0)
    out_ref[...] = pre_ref[...] + above[None]


def write_gradients(kinds, prior, later, refs, *, scale):
    kr_ref, v_ref, o_ref, cos_ref, sin_ref, first_ref, groups_ref, outs, held, sems = refs
    copies = []

    def intra(kind, h):
        for ref, jobs in ((first_ref, BESIDE_FIRST), (groups_ref, BESIDE_GROUPS)):
            if (kind, h) in jobs:
                i = jobs.index((kind, h))
                return ref[:, i * HEAD_DIM : (i + 1) * HEAD_DIM]

    cosine = cos_ref[...] * scale
    sine = sin_ref[...] * scale
    for h in range(HEADS):
        cols = slice(h * HEAD_DIM, (h + 1) * HEAD_DIM)
        for kind in kinds:
            if kind == "dv":
                state = later[cols, :].astype(BF16)
                grad = (intra(kind, h) + dot(kr_ref[:, cols], state, ((1,), (1,)))) * scale
            else:
                rows_ref, state = (o_ref, prior) if kind == "dq" else (v_ref, later)
                grad = intra(kind, h) + dot(rows_ref[:, cols], state[cols, :].astype(BF16), ((1,), (0,)))
                grad = grad * cosine - pltpu.roll(grad, HALF, 1) * sine
            place = KINDS.index(kind)
            held[place][:, cols] = grad.astype(BF16)
            copy = pltpu.make_async_copy(held[place].at[:, cols], outs[place].at[:, cols], sems.at[len(copies)])
            copy.start()
            copies.append(copy)
    for copy in copies:
        copy.wait()


ORDER = [z * 4 + x for z in (4, 5, 6, 7, 0, 1, 2, 3) for x in (2, 3, 0, 1)]
GROUPS = [[2 * p + c for p in ORDER] for c in range(2)]

KINDS = ("dq", "dk", "dv")


def own_kernel(chip_ref, *refs, scale):
    refs = (*refs[:7], refs[7:10], refs[10:13], refs[13])
    core = (lax.axis_index("stretch") & 1)

    @pl.when(core == 0)
    def _():
        write_gradients(("dq",), chip_ref, None, refs, scale=scale)

    @pl.when(core != 0)
    def _():
        write_gradients(("dk", "dv"), None, chip_ref, refs, scale=scale)


def final_kernel(came_ref, *refs, scale):
    refs = (*refs[:7], refs[10:13], refs[13:16], refs[16])
    core = (lax.axis_index("stretch") & 1)

    @pl.when(core == 0)
    def _():
        write_gradients(("dk", "dv"), None, came_ref, refs, scale=scale)

    @pl.when(core != 0)
    def _():
        write_gradients(("dq",), came_ref, None, refs, scale=scale)


def call(kernel, outs, in_specs, cost, out_spec=WHOLE, scratch=(), aliases=None):
    return pl.pallas_call(
        kernel,
        out_shape=tuple(jax.ShapeDtypeStruct(s, d) for s, d in outs),
        in_specs=in_specs,
        out_specs=tuple(out_spec for _ in outs),
        scratch_shapes=scratch,
        input_output_aliases=aliases or {},
        compiler_params=params(),
        cost_estimate=pl.CostEstimate(flops=cost[0], bytes_accessed=cost[1], transcendentals=0),
    )


def shards(queries, keys, values, grad_out, positions):
    ny = lax.axis_size("grp")
    scale = 1.0 / math.sqrt(HEAD_DIM * BLOCK * ny * lax.axis_size("stretch"))
    wide, state, table = (BLOCK, WIDTH), (WIDTH, HEAD_DIM), (BLOCK, HEAD_DIM)
    groups = BLOCK // HEAD_DIM
    qr, kr, v, o, cosine, sine, mine, other = call(
        rotate_kernel,
        [(wide, BF16)] * 4 + [(table, F32)] * 2 + [(state, F32)] * 2,
        [HBM] * 6,
        (2 * 8 * 512 * 128 * 128, 4 << 20),
        scratch=[
            pltpu.VMEM((groups, HEAD_DIM), jnp.int32),
            pltpu.VMEM((1, HEAD_DIM), F32),
            pltpu.VMEM(wide, BF16),
            pltpu.VMEM(wide, BF16),
            pltpu.SemaphoreType.DMA((2,)),
            pltpu.SemaphoreType.DMA((4,)),
        ],
    )(*[
        pltpu.with_memory_space_constraint(a, pltpu.HBM)
        for a in (positions.reshape(groups, HEAD_DIM), jnp.asarray(FREQUENCY), queries, keys, values, grad_out)
    ])

    def intra(jobs, after=()):
        def kernel(*refs):
            intra_kernel(*refs[:4], refs[-1], jobs=jobs)

        shape = (BLOCK, len(jobs) * HEAD_DIM)
        work = 2 * len(jobs) * 2 * BLOCK * BLOCK * HEAD_DIM
        specs = [WHOLE] * (4 + len(after))
        return call(kernel, [(shape, F32)], specs, (work, 3 << 20))(qr, kr, v, o, *after)[0]

    swap = [(i, i ^ 1) for i in range(2 * len(ORDER))]
    chips = len(ORDER)
    piece = (WIDTH // chips, HEAD_DIM)
    came = lax.ppermute(other, "stretch", swap)
    first = intra(BESIDE_FIRST)
    (pair,) = call(pair_kernel, [(state, F32)], [WHOLE] * 3, (0, 1 << 19))(mine, came, first)
    pieces = lax.all_to_all(pair.reshape((chips,) + piece), "stretch", 0, 0, axis_index_groups=GROUPS)
    total, pre = call(
        scan_kernel, [(piece, F32), ((chips,) + piece, F32)], [WHOLE], (0, 1 << 19)
    )(pieces)
    groups = intra(BESIDE_GROUPS, (total,))
    others = [lax.ppermute(total, "grp", [(i, i ^ step) for i in range(ny)]) for step in Y_STEPS]
    (place,) = call(
        place_kernel, [((chips,) + piece, F32)], [WHOLE] * 5, (0, 1 << 19)
    )(pre, *others, groups)
    chip = lax.all_to_all(place, "stretch", 0, 0, axis_index_groups=GROUPS).reshape(state)
    came = lax.ppermute(chip + mine, "stretch", swap)

    def own(*refs):
        own_kernel(*refs, scale=scale)

    def final(*refs):
        final_kernel(*refs, scale=scale)

    held = [pltpu.VMEM(wide, BF16)] * 3 + [pltpu.SemaphoreType.DMA((2 * HEADS,))]
    common = (kr, v, o, cosine, sine, first, groups)
    work = (2 * 4 * 2 * 512 * 128 * 128, 4 << 20)
    begun = call(own, [(wide, BF16)] * 3, [WHOLE] * 8, work, out_spec=HBM, scratch=held)(chip, *common)
    return call(
        final, [(wide, BF16)] * 3, [WHOLE] * 8 + [HBM] * 3, work, out_spec=HBM, scratch=held,
        aliases={8: 0, 9: 1, 10: 2},
    )(came, *common, *begun)


def solution(mesh):
    every = ("grp", "stretch")
    return jax.shard_map(
        shards,
        mesh=mesh,
        in_specs=(P(every, None),) * 4 + (P(every),),
        out_specs=(P(every, None),) * 3,
        check_vma=False,
    )
```

time: 58.3 us -> 53.4 us (0.916)
  blocking collectives: 35.2 us -> 31.4 us
  starting transfers between devices: 11.3 us -> 10.4 us
  waiting for transfers between devices: 0.85 us -> 0.01 us
    all_to_all x2, blocking collectives: 35.2 us -> 31.4 us  [the longest x1 17.8 us: shards(): lax.all_to_all(pair.reshape((chips,) + piece), 'stretch', 0, 0, axis_inde...]
    ppermute x5, starting transfers between devices: 11.3 us -> 10.4 us  [the longest x3 3.78 us: shards(): lax.ppermute(total, 'grp', [(i, i ^ step) for i in range(ny)])]
    pallas_call x3 -> x4, Pallas kernels: 2.04 us -> 2.9 us  [the longest x1 1.43 us: shards(): call(own, [(wide, BF16)] * 3, [WHOLE] * 8, work, out_spec=HBM, scratch=held)]
    ppermute x5, waiting for transfers between devices: 0.85 us -> 0.01 us  [the longest x3 0.01 us: shards(): lax.ppermute(total, 'grp', [(i, i ^ step) for i in range(ny)])]
    pallas_call x3 -> x2, Pallas kernels: 5.03 us -> 4.88 us  [intra(): call(kernel, [(shape, F32)], specs, (work, 3 << 20))(qr, kr, v, o, *after)]
  transfers between devices with their start and end apart: 5 -> 5, of which waited for: 1 -> 0; matrix products, arithmetic and copies ran while one was open for 0% -> 0% of each run, Pallas kernels for 9% -> 12%
where the time goes in v4:
time: 53.4 us; the launch traced here: 53.2 us
  blocking collectives  31.4 us (59%)
  Pallas kernels  10.5 us (20%)
  starting transfers between devices  10.4 us (19%)
  between operations  0.73 us (1%)
    all_to_all x1, blocking collectives, shards(): lax.all_to_all(pair.reshape((chips,) + piece), 'stretch', 0, 0, axis_inde...  17.8 us
    all_to_all x1, blocking collectives, shards(): lax.all_to_all(place, 'stretch', 0, 0, axis_index_groups=GROUPS)  13.7 us
    pallas_call x2, Pallas kernels, intra(): call(kernel, [(shape, F32)], specs, (work, 3 << 20))(qr, kr, v, o, *after)  4.88 us
    ppermute x3, starting transfers between devices, shards(): lax.ppermute(total, 'grp', [(i, i ^ step) for i in range(ny)])  3.78 us
    ppermute x1, starting transfers between devices, shards(): came = lax.ppermute(chip + mine, 'stretch', swap)  3.34 us
    ppermute x1, starting transfers between devices, shards(): came = lax.ppermute(other, 'stretch', swap)  3.33 us
    pallas_call x1, Pallas kernels, shards(): call(rotate_kernel, [(wide, BF16)] * 4 + [(table, F32)] * 2 + [(state, F3...  2.72 us
    pallas_call x1, Pallas kernels, shards(): call(own, [(wide, BF16)] * 3, [WHOLE] * 8, work, out_spec=HBM, scratch=held)  1.43 us
  transfers between devices with their start and end apart: 5, of which 0 were waited for; matrix products, arithmetic and copies ran while one was open for 0% of the time, Pallas kernels for 12%

profile of v4, /device:TPU:1, one launch (start us, length us, event | category | flops | bytes accessed | tf_op | source)
XLA Modules:
  0.0 53.2 jit_solution(12236692642854864235)
XLA Ops:
  0.6 2.7 %shard_map.85 = (bf16[512,512]{1,0:T(8,128)(2,1)S(1)}, bf16[512,512]{1,0:T(8,128)(2,1)S(1)}, bf16[512,512]{1,0:T(8,128)(2,1)S(1)}, bf16[512,512]{1,0:T(8,128)(2,...) custom-call(s32[4,128]{1,0:T(4,128)} %bitcast.6, ...), custom_call_target="tpu_custom_call" | custom-call | flops 134217728 | bytes 4194304 | tf_op jit(solution)/shard_map/pallas_call | solution.py:265
  3.4 3.3 %collective-permute-start = (f32[512,128]{1,0:T(8,128)S(1)}, f32[512,128]{1,0:T(8,128)S(1)}, u32[]{:S(2)}, u32[]{:S(2)}) collective-permute-start(f32[512,128]{1,0:T(8,128)S(1)} %get-tuple-element.17), channel_id=1, source_target_pairs={{0,1},{1,0},{2,3},{3,2},{4,5},{5,4},{6,7},{7,6},{8,9},{9,8},{10,11... | collective-permute-start | bytes 786440 | tf_op jit(solution)/shard_map/ppermute | solution.py:295
  6.7 1.3 %shard_map.86._.refs_6_ = f32[512,384]{1,0:T(8,128)S(1)} custom-call(bf16[512,512]{1,0:T(8,128)(2,1)S(1)} %get-tuple-element.18.refs_0_, bf16[512,512]{1,0:T(8,128)(2,1)S(1)} %get-tuple-element.19.refs_1_, bf16[512,512]{1,0:T(8,128)(2,1)S(1)} %get-tuple-element.20.refs_2_, bf16[512,512]{1,0:T(8,128)(2,1)S(1)} %get-tuple-element.21.refs_3_), custom_call_target="tpu_custom_call" | custom-call | flops 402653184 | bytes 3145728 | tf_op jit(solution)/shard_map/pallas_call | solution.py:290
  8.0 0.0 collective-permute-done.came_ref
  8.1 17.8 %all_to_all.10.r_ref = f32[32,16,128]{2,1,0:T(8,128)S(1)} all-to-all(f32[32,16,128]{2,1,0:T(8,128)S(1)} %bitcast.5), channel_id=1, replica_groups={{36,38,32,34,44,46,40,42,52,54,48,50,60,62,56,58,4,6,0,2,12,14,8,10,20,..., dimensions={0} | all-to-all | bytes 524288 | tf_op jit(solution)/shard_map/all_to_all | solution.py:298
  25.8 0.1 shard_map.88
  25.9 3.0 %collective-permute-start.3 = (f32[16,128]{1,0:T(8,128)S(1)}, f32[16,128]{1,0:T(8,128)S(1)}, u32[]{:S(2)}, u32[]{:S(2)}) collective-permute-start(f32[16,128]{1,0:T(8,128)S(1)} %get-tuple-element.23.refs_4_), channel_id=1, source_target_pairs={{0,128},{64,192},{128,0},{192,64},{1,129},{65,193},{129,1},{193,65... | collective-permute-start | bytes 24584 | tf_op jit(solution)/shard_map/ppermute | solution.py:303
  28.9 0.8 %collective-permute-start.2 = (f32[16,128]{1,0:T(8,128)S(1)}, f32[16,128]{1,0:T(8,128)S(1)}, u32[]{:S(2)}, u32[]{:S(2)}) collective-permute-start(f32[16,128]{1,0:T(8,128)S(1)} %get-tuple-element.23.refs_4_), channel_id=1, source_target_pairs={{0,192},{64,128},{128,64},{192,0},{1,193},{65,129},{129,65},{193,1... | collective-permute-start | bytes 24584 | tf_op jit(solution)/shard_map/ppermute | solution.py:303
  29.7 0.0 collective-permute-start.1
  29.7 3.6 %shard_map.89._.refs_7_ = f32[512,1152]{1,0:T(8,128)S(1)} custom-call(bf16[512,512]{1,0:T(8,128)(2,1)S(1)} %get-tuple-element.18.refs_0_, bf16[512,512]{1,0:T(8,128)(2,1)S(1)} %get-tuple-element.19.refs_1_, bf16[512,512]{1,0:T(8,128)(2,1)S(1)} %get-tuple-element.20.refs_2_, bf16[512,512]{1,0:T(8,128)(2,1)S(1)} %get-tuple-element.21.refs_3_, ...), custom_call_target="tpu_custom_call" | custom-call | flops 1207959552 | bytes 3145728 | tf_op jit(solution)/shard_map/pallas_call | solution.py:290
  33.3 0.0 collective-permute-done.3.c_ref
  33.3 0.0 collective-permute-done.2.b_ref
  33.3 0.0 collective-permute-done.1.a_ref
  33.3 13.7 %all_to_all.11 = f32[32,16,128]{2,1,0:T(8,128)S(1)} all-to-all(f32[32,16,128]{2,1,0:T(8,128)S(1)} %shard_map.90), channel_id=1, replica_groups={{36,38,32,34,44,46,40,42,52,54,48,50,60,62,56,58,4,6,0,2,12,14,8,10,20,..., dimensions={0} | all-to-all | bytes 524288 | tf_op jit(solution)/shard_map/all_to_all | solution.py:307
  47.0 3.3 %collective-permute-start.4 = (f32[512,128]{1,0:T(8,128)S(1)}, f32[512,128]{1,0:T(8,128)S(1)}, u32[]{:S(2)}, u32[]{:S(2)}) collective-permute-start(f32[512,128]{1,0:T(8,128)S(1)} %bitcast_add_fusion), channel_id=1, source_target_pairs={{0,1},{1,0},{2,3},{3,2},{4,5},{5,4},{6,7},{7,6},{8,9},{9,8},{10,11... | collective-permute-start | bytes 786440 | tf_op jit(solution)/shard_map/ppermute | solution.py:308
  50.4 1.4 %shard_map.91 = (bf16[512,512]{1,0:T(8,128)(2,1)}, bf16[512,512]{1,0:T(8,128)(2,1)}, bf16[512,512]{1,0:T(8,128)(2,1)}) custom-call(f32[512,128]{1,0:T(8,128)S(1)} %bitcast.4, bf16[512,512]{1,0:T(8,128)(2,1)S(1)} %get-tuple-element.19.refs_1_, bf16[512,512]{1,0:T(8,128)(2,1)S(1)} %get-tuple-element.20.refs_2_, ...), custom_call_target="tpu_custom_call" | custom-call | flops 134217728 | bytes 4194304 | tf_op jit(solution)/shard_map/pallas_call | solution.py:319
  51.8 0.0 collective-permute-done.4.refs_0_
  51.8 1.4 %shard_map.92 = (bf16[512,512]{1,0:T(8,128)(2,1)}, bf16[512,512]{1,0:T(8,128)(2,1)}, bf16[512,512]{1,0:T(8,128)(2,1)}) custom-call(f32[512,128]{1,0:T(8,128)S(1)} %collective-permute-done.4.refs_0_, bf16[512,512]{1,0:T(8,128)(2,1)S(1)} %get-tuple-element.19.refs_1_, ...), custom_call_target="tpu_custom_call", output_to_operand_aliasing={{0}: (8, {}), {1}: (9, {}), {2}: (10, {})} | custom-call | flops 134217728 | bytes 4194304 | tf_op jit(solution)/shard_map/pallas_call | solution.py:320
  (3 shorter events, 0.1 us)
Async XLA Ops:
  3.4 4.7 %collective-permute-start = (f32[512,128]{1,0:T(8,128)S(1)}, f32[512,128]{1,0:T(8,128)S(1)}, u32[]{:S(2)}, u32[]{:S(2)}) collective-permute-start(f32[512,128]{1,0:T(8,128)S(1)} %get-tuple-element.17), channel_id=1, source_target_pairs={{0,1},{1,0},{2,3},{3,2},{4,5},{5,4},{6,7},{7,6},{8,9},{9,8},{10,11... | collective-permute-start | bytes 786440 | tf_op jit(solution)/shard_map/ppermute | solution.py:295
  25.9 7.3 %collective-permute-start.3 = (f32[16,128]{1,0:T(8,128)S(1)}, f32[16,128]{1,0:T(8,128)S(1)}, u32[]{:S(2)}, u32[]{:S(2)}) collective-permute-start(f32[16,128]{1,0:T(8,128)S(1)} %get-tuple-element.23.refs_4_), channel_id=1, source_target_pairs={{0,128},{64,192},{128,0},{192,64},{1,129},{65,193},{129,1},{193,65... | collective-permute-start | bytes 24584 | tf_op jit(solution)/shard_map/ppermute | solution.py:303
  28.9 4.4 %collective-permute-start.2 = (f32[16,128]{1,0:T(8,128)S(1)}, f32[16,128]{1,0:T(8,128)S(1)}, u32[]{:S(2)}, u32[]{:S(2)}) collective-permute-start(f32[16,128]{1,0:T(8,128)S(1)} %get-tuple-element.23.refs_4_), channel_id=1, source_target_pairs={{0,192},{64,128},{128,64},{192,0},{1,193},{65,129},{129,65},{193,1... | collective-permute-start | bytes 24584 | tf_op jit(solution)/shard_map/ppermute | solution.py:303
  29.7 3.6 %collective-permute-start.1 = (f32[16,128]{1,0:T(8,128)S(1)}, f32[16,128]{1,0:T(8,128)S(1)}, u32[]{:S(2)}, u32[]{:S(2)}) collective-permute-start(f32[16,128]{1,0:T(8,128)S(1)} %get-tuple-element.23.refs_4_), channel_id=1, source_target_pairs={{0,64},{64,0},{128,192},{192,128},{1,65},{65,1},{129,193},{193,129... | collective-permute-start | bytes 24584 | tf_op jit(solution)/shard_map/ppermute | solution.py:303
  47.0 4.8 %collective-permute-start.4 = (f32[512,128]{1,0:T(8,128)S(1)}, f32[512,128]{1,0:T(8,128)S(1)}, u32[]{:S(2)}, u32[]{:S(2)}) collective-permute-start(f32[512,128]{1,0:T(8,128)S(1)} %bitcast_add_fusion), channel_id=1, source_target_pairs={{0,1},{1,0},{2,3},{3,2},{4,5},{5,4},{6,7},{7,6},{8,9},{9,8},{10,11... | collective-permute-start | bytes 786440 | tf_op jit(solution)/shard_map/ppermute | solution.py:308

commit v5 on v4

--- a/solution.py
+++ b/solution.py
@@ -57,7 +57,7 @@
     qr_ref, kr_ref, v_ref, o_ref, cos_ref, sin_ref, mine_ref, other_ref,
     pos_ref, freq_ref, q_ref, k_ref, small_sems, sems,
 ):
-    core = (lax.axis_index("stretch") & 1)
+    keys_here = on_keys()
     small = [
         pltpu.make_async_copy(pos_hbm, pos_ref, small_sems.at[0]),
         pltpu.make_async_copy(freq_hbm, freq_ref, small_sems.at[1]),
@@ -102,8 +102,28 @@
     query_states = rotated(q_ref, qr_ref, o_ref)
     for h in range(HEADS):
         rows = slice(h * HEAD_DIM, (h + 1) * HEAD_DIM)
-        mine_ref[rows, :] = jnp.where(core == 0, mine_ref[rows, :], query_states[h])
-        other_ref[rows, :] = jnp.where(core == 0, query_states[h], other_ref[rows, :])
+        mine_ref[rows, :] = jnp.where(keys_here, mine_ref[rows, :], query_states[h])
+        other_ref[rows, :] = jnp.where(keys_here, query_states[h], other_ref[rows, :])
+
+
+FLIPPED = (18,)
+ORDER = (
+    [(18 + i) % 32 for i in range(32)],
+    [(22 + i) % 32 for i in range(32)],
+)
+GROUPS = [[2 * p + (side ^ (p in FLIPPED)) for p in ORDER[side]] for side in range(2)]
+
+
+def flipped():
+    chip = lax.axis_index("stretch") // 2
+    found = chip == FLIPPED[0]
+    for p in FLIPPED[1:]:
+        found = jnp.logical_or(found, chip == p)
+    return found
+
+
+def on_keys():
+    return ((lax.axis_index("stretch") & 1) == 0) != flipped()
 
 
 def triangle(a_ref, b_ref, c_ref, h, low):
@@ -126,11 +146,13 @@
 
 
 BESIDE_FIRST = (("dv", 0), ("dv", 1), ("dv", 2))
-BESIDE_GROUPS = tuple(("dq", h) for h in range(HEADS)) + tuple(("dk", h) for h in range(HEADS)) + (("dv", 3),)
+BESIDE_GROUPS = tuple(("dq", h) for h in range(HEADS)) + (("dv", 3),)
+EXTRA = tuple(("dk", h) for h in range(HEADS))
 Y_STEPS = (1, 3, 2)
 
 
-def intra_kernel(qr_ref, kr_ref, v_ref, o_ref, out_ref, *, jobs):
+def run_jobs(jobs, refs, out_ref):
+    qr_ref, kr_ref, v_ref, o_ref = refs
     n = BLOCK // 2
     for i, (kind, h) in enumerate(jobs):
         cols = slice(i * HEAD_DIM, (i + 1) * HEAD_DIM)
@@ -144,26 +166,48 @@
         out_ref[n:, cols] = low
 
 
+def early():
+    return lax.axis_index("stretch") < len(ORDER[0]) // 2
+
+
+def first_kernel(*refs):
+    run_jobs(BESIDE_FIRST, refs[:4], refs[4])
+
+    @pl.when(early())
+    def _():
+        run_jobs(EXTRA, refs[:4], refs[5])
+
+
+def groups_kernel(*refs):
+    run_jobs(BESIDE_GROUPS, refs[:4], refs[5])
+
+
+def last_kernel(*refs):
+    @pl.when(jnp.logical_not(early()))
+    def _():
+        run_jobs(EXTRA, refs[:4], refs[6])
+
+
 def scan_kernel(r_ref, total_ref, pre_ref):
     n = r_ref.shape[0]
-    token_order = sorted(range(n), key=lambda i: ORDER[i])
+    before, after = (sorted(range(n), key=lambda i: order[i]) for order in ORDER)
     total = r_ref[0]
     for i in range(1, n):
         total = total + r_ref[i]
     total_ref[...] = total
-    up = (lax.axis_index("stretch") & 1) == 0
+    up = on_keys()
 
     @pl.when(up)
     def _():
         acc = jnp.zeros_like(total)
-        for i in token_order:
+        for i in before:
             pre_ref[i] = acc
             acc = acc + r_ref[i]
 
     @pl.when(jnp.logical_not(up))
     def _():
         acc = jnp.zeros_like(total)
-        for i in reversed(token_order):
+        for i in reversed(after):
             pre_ref[i] = acc
             acc = acc + r_ref[i]
 
@@ -172,9 +216,15 @@
     out_ref[...] = mine_ref[...] + came_ref[...]
 
 
+def own_state_kernel(chip_ref, mine_ref, came_ref, own_ref, sent_ref):
+    turned = flipped()
+    own_ref[...] = chip_ref[...] + jnp.where(turned, came_ref[...], 0.0)
+    sent_ref[...] = chip_ref[...] + jnp.where(turned, 0.0, mine_ref[...])
+
+
 def place_kernel(pre_ref, a_ref, b_ref, c_ref, _, out_ref):
     above = jnp.zeros(a_ref.shape, F32)
-    up, y = (lax.axis_index("stretch") & 1) == 0, lax.axis_index("grp")
+    up, y = on_keys(), lax.axis_index("grp")
     for step, ref in zip(Y_STEPS, (a_ref, b_ref, c_ref)):
         below = (y ^ step) < y
         above = above + jnp.where(up == below, ref[...], 0.0)
@@ -182,11 +232,11 @@
 
 
 def write_gradients(kinds, prior, later, refs, *, scale):
-    kr_ref, v_ref, o_ref, cos_ref, sin_ref, first_ref, groups_ref, outs, held, sems = refs
+    kr_ref, v_ref, o_ref, cos_ref, sin_ref, first_ref, groups_ref, extra_ref, outs, held, sems = refs
     copies = []
 
     def intra(kind, h):
-        for ref, jobs in ((first_ref, BESIDE_FIRST), (groups_ref, BESIDE_GROUPS)):
+        for ref, jobs in ((first_ref, BESIDE_FIRST), (groups_ref, BESIDE_GROUPS), (extra_ref, EXTRA)):
             if (kind, h) in jobs:
                 i = jobs.index((kind, h))
                 return ref[:, i * HEAD_DIM : (i + 1) * HEAD_DIM]
@@ -212,34 +262,31 @@
         copy.wait()
 
 
-ORDER = [z * 4 + x for z in (4, 5, 6, 7, 0, 1, 2, 3) for x in (2, 3, 0, 1)]
-GROUPS = [[2 * p + c for p in ORDER] for c in range(2)]
-
 KINDS = ("dq", "dk", "dv")
 
 
 def own_kernel(chip_ref, *refs, scale):
-    refs = (*refs[:7], refs[7:10], refs[10:13], refs[13])
-    core = (lax.axis_index("stretch") & 1)
-
-    @pl.when(core == 0)
+    refs = (*refs[:8], refs[8:11], refs[11:14], refs[14])
+    keys_here = on_keys()
+
+    @pl.when(keys_here)
     def _():
         write_gradients(("dq",), chip_ref, None, refs, scale=scale)
 
-    @pl.when(core != 0)
+    @pl.when(jnp.logical_not(keys_here))
     def _():
         write_gradients(("dk", "dv"), None, chip_ref, refs, scale=scale)
 
 
 def final_kernel(came_ref, *refs, scale):
-    refs = (*refs[:7], refs[10:13], refs[13:16], refs[16])
-    core = (lax.axis_index("stretch") & 1)
-
-    @pl.when(core == 0)
+    refs = (*refs[:8], refs[11:14], refs[14:17], refs[17])
+    keys_here = on_keys()
+
+    @pl.when(keys_here)
     def _():
         write_gradients(("dk", "dv"), None, came_ref, refs, scale=scale)
 
-    @pl.when(core != 0)
+    @pl.when(jnp.logical_not(keys_here))
     def _():
         write_gradients(("dq",), came_ref, None, refs, scale=scale)
 
@@ -280,32 +327,38 @@
         for a in (positions.reshape(groups, HEAD_DIM), jnp.asarray(FREQUENCY), queries, keys, values, grad_out)
     ])
 
-    def intra(jobs, after=()):
-        def kernel(*refs):
-            intra_kernel(*refs[:4], refs[-1], jobs=jobs)
-
-        shape = (BLOCK, len(jobs) * HEAD_DIM)
-        work = 2 * len(jobs) * 2 * BLOCK * BLOCK * HEAD_DIM
-        specs = [WHOLE] * (4 + len(after))
-        return call(kernel, [(shape, F32)], specs, (work, 3 << 20))(qr, kr, v, o, *after)[0]
-
-    swap = [(i, i ^ 1) for i in range(2 * len(ORDER))]
-    chips = len(ORDER)
+    def work(*jobs):
+        return (2 * sum(map(len, jobs)) * 2 * BLOCK * BLOCK * HEAD_DIM, 3 << 20)
+
+    def products(*jobs):
+        return [((BLOCK, len(each) * HEAD_DIM), F32) for each in jobs]
+
+    swap = [(i, i ^ 1) for i in range(2 * len(ORDER[0]))]
+    chips = len(ORDER[0])
     piece = (WIDTH // chips, HEAD_DIM)
     came = lax.ppermute(other, "stretch", swap)
-    first = intra(BESIDE_FIRST)
+    rows = (qr, kr, v, o)
+    first, extra = call(
+        first_kernel, products(BESIDE_FIRST, EXTRA), [WHOLE] * 4, work(BESIDE_FIRST)
+    )(*rows)
     (pair,) = call(pair_kernel, [(state, F32)], [WHOLE] * 3, (0, 1 << 19))(mine, came, first)
     pieces = lax.all_to_all(pair.reshape((chips,) + piece), "stretch", 0, 0, axis_index_groups=GROUPS)
     total, pre = call(
         scan_kernel, [(piece, F32), ((chips,) + piece, F32)], [WHOLE], (0, 1 << 19)
     )(pieces)
-    groups = intra(BESIDE_GROUPS, (total,))
+    (groups,) = call(
+        groups_kernel, products(BESIDE_GROUPS), [WHOLE] * 5, work(BESIDE_GROUPS)
+    )(*rows, total)
     others = [lax.ppermute(total, "grp", [(i, i ^ step) for i in range(ny)]) for step in Y_STEPS]
     (place,) = call(
         place_kernel, [((chips,) + piece, F32)], [WHOLE] * 5, (0, 1 << 19)
     )(pre, *others, groups)
     chip = lax.all_to_all(place, "stretch", 0, 0, axis_index_groups=GROUPS).reshape(state)
-    came = lax.ppermute(chip + mine, "stretch", swap)
+    own_state, sent = call(own_state_kernel, [(state, F32)] * 2, [WHOLE] * 3, (0, 1 << 19))(chip, mine, came)
+    came = lax.ppermute(sent, "stretch", swap)
+    (extra,) = call(
+        last_kernel, products(EXTRA), [WHOLE] * 6, work(EXTRA), aliases={5: 0}
+    )(*rows, chip, extra)
 
     def own(*refs):
         own_kernel(*refs, scale=scale)
@@ -314,12 +367,12 @@
         final_kernel(*refs, scale=scale)
 
     held = [pltpu.VMEM(wide, BF16)] * 3 + [pltpu.SemaphoreType.DMA((2 * HEADS,))]
-    common = (kr, v, o, cosine, sine, first, groups)
-    work = (2 * 4 * 2 * 512 * 128 * 128, 4 << 20)
-    begun = call(own, [(wide, BF16)] * 3, [WHOLE] * 8, work, out_spec=HBM, scratch=held)(chip, *common)
+    common = (kr, v, o, cosine, sine, first, groups, extra)
+    cost = (2 * 4 * 2 * 512 * 128 * 128, 4 << 20)
+    begun = call(own, [(wide, BF16)] * 3, [WHOLE] * 9, cost, out_spec=HBM, scratch=held)(own_state, *common)
     return call(
-        final, [(wide, BF16)] * 3, [WHOLE] * 8 + [HBM] * 3, work, out_spec=HBM, scratch=held,
-        aliases={8: 0, 9: 1, 10: 2},
+        final, [(wide, BF16)] * 3, [WHOLE] * 9 + [HBM] * 3, cost, out_spec=HBM, scratch=held,
+        aliases={9: 0, 10: 1, 11: 2},
     )(came, *common, *begun)
 
 

time: 53.4 us -> 52.7 us (0.987)
  blocking collectives: 31.4 us -> 29.5 us
  waiting for transfers between devices: 0.01 us -> 0.99 us
    all_to_all x1, blocking collectives: 17.8 us -> 15.7 us  [shards(): lax.all_to_all(pair.reshape((chips,) + piece), 'stretch', 0, 0, axis_inde...]
    ppermute x3, waiting for transfers between devices: 0.01 us -> 0.98 us  [shards(): lax.ppermute(total, 'grp', [(i, i ^ step) for i in range(ny)])]
    pallas_call x4 -> x6, Pallas kernels: 7.67 us -> 7.83 us  [the longest x1 3.04 us: shards(): call(first_kernel, products(BESIDE_FIRST, EXTRA), [WHOLE] * 4, work(BESID...]
  transfers between devices with their start and end apart: 5 -> 5, of which waited for: 0 -> 1; matrix products, arithmetic and copies ran while one was open for 0% -> 0% of each run, Pallas kernels for 12% -> 12%
where the time goes in v5:
time: 52.7 us; the launch traced here: 52.5 us
  blocking collectives  29.5 us (56%)
  Pallas kernels  10.7 us (20%)
  starting transfers between devices  10.6 us (20%)
  waiting for transfers between devices  0.99 us (2%)
  between operations  0.71 us (1%)
    all_to_all x1, blocking collectives, shards(): lax.all_to_all(pair.reshape((chips,) + piece), 'stretch', 0, 0, axis_inde...  15.7 us
    all_to_all x1, blocking collectives, shards(): lax.all_to_all(place, 'stretch', 0, 0, axis_index_groups=GROUPS)  13.8 us
    ppermute x3, starting transfers between devices, shards(): lax.ppermute(total, 'grp', [(i, i ^ step) for i in range(ny)])  3.78 us
    ppermute x1, starting transfers between devices, shards(): came = lax.ppermute(sent, 'stretch', swap)  3.54 us
    ppermute x1, starting transfers between devices, shards(): came = lax.ppermute(other, 'stretch', swap)  3.33 us
    pallas_call x1, Pallas kernels, shards(): call(first_kernel, products(BESIDE_FIRST, EXTRA), [WHOLE] * 4, work(BESID...  3.04 us
    pallas_call x1, Pallas kernels, shards(): call(rotate_kernel, [(wide, BF16)] * 4 + [(table, F32)] * 2 + [(state, F3...  2.7 us
    pallas_call x1, Pallas kernels, shards(): call(groups_kernel, products(BESIDE_GROUPS), [WHOLE] * 5, work(BESIDE_GRO...  1.95 us
  transfers between devices with their start and end apart: 5, of which 1 were waited for; matrix products, arithmetic and copies ran while one was open for 0% of the time, Pallas kernels for 12%

profile of v5, /device:TPU:1, one launch (start us, length us, event | category | flops | bytes accessed | tf_op | source)
XLA Modules:
  0.0 52.5 jit_solution(6503559503594433181)
XLA Ops:
  0.6 2.7 %shard_map.85 = (bf16[512,512]{1,0:T(8,128)(2,1)S(1)}, bf16[512,512]{1,0:T(8,128)(2,1)S(1)}, bf16[512,512]{1,0:T(8,128)(2,1)S(1)}, bf16[512,512]{1,0:T(8,128)(2,...) custom-call(s32[4,128]{1,0:T(4,128)} %bitcast.6, ...), custom_call_target="tpu_custom_call" | custom-call | flops 134217728 | bytes 4194304 | tf_op jit(solution)/shard_map/pallas_call | solution.py:312
  3.3 3.3 %collective-permute-start = (f32[512,128]{1,0:T(8,128)S(1)}, f32[512,128]{1,0:T(8,128)S(1)}, u32[]{:S(2)}, u32[]{:S(2)}) collective-permute-start(f32[512,128]{1,0:T(8,128)S(1)} %get-tuple-element.21), channel_id=1, source_target_pairs={{0,1},{1,0},{2,3},{3,2},{4,5},{5,4},{6,7},{7,6},{8,9},{9,8},{10,11... | collective-permute-start | bytes 786440 | tf_op jit(solution)/shard_map/ppermute | solution.py:339
  6.7 3.0 %shard_map.86 = (f32[512,384]{1,0:T(8,128)S(1)}, f32[512,512]{1,0:T(8,128)S(1)}) custom-call(bf16[512,512]{1,0:T(8,128)(2,1)S(1)} %get-tuple-element.22.refs_0_, bf16[512,512]{1,0:T(8,128)(2,1)S(1)} %get-tuple-element.23.refs_1_, bf16[512,512]{1,0:T(8,128)(2,1)S(1)} %get-tuple-element.24.refs_2_, bf16[512,512]{1,0:T(8,128)(2,1)S(1)} %get-tuple-element.25.refs_3_), custom_call_target="tpu_custom_call" | custom-call | flops 402653184 | bytes 3145728 | tf_op jit(solution)/shard_map/pallas_call | solution.py:341
  9.7 0.0 collective-permute-done.came_ref
  9.8 15.7 %all_to_all.10.r_ref = f32[32,16,128]{2,1,0:T(8,128)S(1)} all-to-all(f32[32,16,128]{2,1,0:T(8,128)S(1)} %bitcast.5), channel_id=1, replica_groups={{37,38,40,42,44,46,48,50,52,54,56,58,60,62,0,2,4,6,8,10,12,14,16,18,20,..., dimensions={0} | all-to-all | bytes 524288 | tf_op jit(solution)/shard_map/all_to_all | solution.py:345
  25.5 0.1 shard_map.88
  25.6 3.0 %collective-permute-start.3 = (f32[16,128]{1,0:T(8,128)S(1)}, f32[16,128]{1,0:T(8,128)S(1)}, u32[]{:S(2)}, u32[]{:S(2)}) collective-permute-start(f32[16,128]{1,0:T(8,128)S(1)} %get-tuple-element.28.refs_4_), channel_id=1, source_target_pairs={{0,128},{64,192},{128,0},{192,64},{1,129},{65,193},{129,1},{193,65... | collective-permute-start | bytes 24584 | tf_op jit(solution)/shard_map/ppermute | solution.py:352
  28.6 0.8 %collective-permute-start.2 = (f32[16,128]{1,0:T(8,128)S(1)}, f32[16,128]{1,0:T(8,128)S(1)}, u32[]{:S(2)}, u32[]{:S(2)}) collective-permute-start(f32[16,128]{1,0:T(8,128)S(1)} %get-tuple-element.28.refs_4_), channel_id=1, source_target_pairs={{0,192},{64,128},{128,64},{192,0},{1,193},{65,129},{129,65},{193,1... | collective-permute-start | bytes 24584 | tf_op jit(solution)/shard_map/ppermute | solution.py:352
  29.4 0.0 collective-permute-start.1
  29.4 2.0 %shard_map.89._.refs_7_ = f32[512,640]{1,0:T(8,128)S(1)} custom-call(bf16[512,512]{1,0:T(8,128)(2,1)S(1)} %get-tuple-element.22.refs_0_, bf16[512,512]{1,0:T(8,128)(2,1)S(1)} %get-tuple-element.23.refs_1_, bf16[512,512]{1,0:T(8,128)(2,1)S(1)} %get-tuple-element.24.refs_2_, bf16[512,512]{1,0:T(8,128)(2,1)S(1)} %get-tuple-element.25.refs_3_, ...), custom_call_target="tpu_custom_call" | custom-call | flops 671088640 | bytes 3145728 | tf_op jit(solution)/shard_map/pallas_call | solution.py:349
  31.3 0.0 collective-permute-done.3.c_ref
  31.3 1.0 %collective-permute-done.2.b_ref = f32[16,128]{1,0:T(8,128)S(1)} collective-permute-done((f32[16,128]{1,0:T(8,128)S(1)}, f32[16,128]{1,0:T(8,128)S(1)}, u32[]{:S(2)}, u32[]{:S(2)}) %collective-permute-start.2) | collective-permute-done | bytes 8224 | tf_op jit(solution)/shard_map/ppermute | solution.py:352
  32.3 0.0 collective-permute-done.1.a_ref
  32.4 13.8 %all_to_all.11 = f32[32,16,128]{2,1,0:T(8,128)S(1)} all-to-all(f32[32,16,128]{2,1,0:T(8,128)S(1)} %shard_map.90), channel_id=1, replica_groups={{37,38,40,42,44,46,48,50,52,54,56,58,60,62,0,2,4,6,8,10,12,14,16,18,20,..., dimensions={0} | all-to-all | bytes 524288 | tf_op jit(solution)/shard_map/all_to_all | solution.py:356
  46.1 0.1 shard_map.91
  46.2 3.5 %collective-permute-start.4 = (f32[512,128]{1,0:T(8,128)S(1)}, f32[512,128]{1,0:T(8,128)S(1)}, u32[]{:S(2)}, u32[]{:S(2)}) collective-permute-start(f32[512,128]{1,0:T(8,128)S(1)} %get-tuple-element.29), channel_id=1, source_target_pairs={{0,1},{1,0},{2,3},{3,2},{4,5},{5,4},{6,7},{7,6},{8,9},{9,8},{10,11... | collective-permute-start | bytes 786440 | tf_op jit(solution)/shard_map/ppermute | solution.py:358
  49.8 1.4 %shard_map.93 = (bf16[512,512]{1,0:T(8,128)(2,1)}, bf16[512,512]{1,0:T(8,128)(2,1)}, bf16[512,512]{1,0:T(8,128)(2,1)}) custom-call(f32[512,128]{1,0:T(8,128)S(1)} %get-tuple-element.33.refs_0_, bf16[512,512]{1,0:T(8,128)(2,1)S(1)} %get-tuple-element.23.refs_1_, bf16[512,512]{1,0:T(8,128)(2,1)S(1)} %get-tuple-element.24.refs_2_, ...), custom_call_target="tpu_custom_call" | custom-call | flops 134217728 | bytes 4194304 | tf_op jit(solution)/shard_map/pallas_call | solution.py:372
  51.2 0.0 collective-permute-done.4.refs_0_
  51.2 1.4 %shard_map.94 = (bf16[512,512]{1,0:T(8,128)(2,1)}, bf16[512,512]{1,0:T(8,128)(2,1)}, bf16[512,512]{1,0:T(8,128)(2,1)}) custom-call(f32[512,128]{1,0:T(8,128)S(1)} %collective-permute-done.4.refs_0_, bf16[512,512]{1,0:T(8,128)(2,1)S(1)} %get-tuple-element.23.refs_1_, ...), custom_call_target="tpu_custom_call", output_to_operand_aliasing={{0}: (9, {}), {1}: (10, {}), {2}: (11, {})} | custom-call | flops 134217728 | bytes 4194304 | tf_op jit(solution)/shard_map/pallas_call | solution.py:373
  (3 shorter events, 0.1 us)
Async XLA Ops:
  3.3 6.4 %collective-permute-start = (f32[512,128]{1,0:T(8,128)S(1)}, f32[512,128]{1,0:T(8,128)S(1)}, u32[]{:S(2)}, u32[]{:S(2)}) collective-permute-start(f32[512,128]{1,0:T(8,128)S(1)} %get-tuple-element.21), channel_id=1, source_target_pairs={{0,1},{1,0},{2,3},{3,2},{4,5},{5,4},{6,7},{7,6},{8,9},{9,8},{10,11... | collective-permute-start | bytes 786440 | tf_op jit(solution)/shard_map/ppermute | solution.py:339
  25.6 5.7 %collective-permute-start.3 = (f32[16,128]{1,0:T(8,128)S(1)}, f32[16,128]{1,0:T(8,128)S(1)}, u32[]{:S(2)}, u32[]{:S(2)}) collective-permute-start(f32[16,128]{1,0:T(8,128)S(1)} %get-tuple-element.28.refs_4_), channel_id=1, source_target_pairs={{0,128},{64,192},{128,0},{192,64},{1,129},{65,193},{129,1},{193,65... | collective-permute-start | bytes 24584 | tf_op jit(solution)/shard_map/ppermute | solution.py:352
  28.6 3.7 %collective-permute-start.2 = (f32[16,128]{1,0:T(8,128)S(1)}, f32[16,128]{1,0:T(8,128)S(1)}, u32[]{:S(2)}, u32[]{:S(2)}) collective-permute-start(f32[16,128]{1,0:T(8,128)S(1)} %get-tuple-element.28.refs_4_), channel_id=1, source_target_pairs={{0,192},{64,128},{128,64},{192,0},{1,193},{65,129},{129,65},{193,1... | collective-permute-start | bytes 24584 | tf_op jit(solution)/shard_map/ppermute | solution.py:352
  29.4 3.0 %collective-permute-start.1 = (f32[16,128]{1,0:T(8,128)S(1)}, f32[16,128]{1,0:T(8,128)S(1)}, u32[]{:S(2)}, u32[]{:S(2)}) collective-permute-start(f32[16,128]{1,0:T(8,128)S(1)} %get-tuple-element.28.refs_4_), channel_id=1, source_target_pairs={{0,64},{64,0},{128,192},{192,128},{1,65},{65,1},{129,193},{193,129... | collective-permute-start | bytes 24584 | tf_op jit(solution)/shard_map/ppermute | solution.py:352
  46.2 5.0 %collective-permute-start.4 = (f32[512,128]{1,0:T(8,128)S(1)}, f32[512,128]{1,0:T(8,128)S(1)}, u32[]{:S(2)}, u32[]{:S(2)}) collective-permute-start(f32[512,128]{1,0:T(8,128)S(1)} %get-tuple-element.29), channel_id=1, source_target_pairs={{0,1},{1,0},{2,3},{3,2},{4,5},{5,4},{6,7},{7,6},{8,9},{9,8},{10,11... | collective-permute-start | bytes 786440 | tf_op jit(solution)/shard_map/ppermute | solution.py:358

commit v6 on v5

--- a/solution.py
+++ b/solution.py
@@ -185,7 +185,7 @@
 def last_kernel(*refs):
     @pl.when(jnp.logical_not(early()))
     def _():
-        run_jobs(EXTRA, refs[:4], refs[6])
+        run_jobs(EXTRA, refs[:4], refs[5])
 
 
 def scan_kernel(r_ref, total_ref, pre_ref):
@@ -232,14 +232,17 @@
 
 
 def write_gradients(kinds, prior, later, refs, *, scale):
-    kr_ref, v_ref, o_ref, cos_ref, sin_ref, first_ref, groups_ref, extra_ref, outs, held, sems = refs
+    kr_ref, v_ref, o_ref, cos_ref, sin_ref, first_ref, groups_ref, soon_ref, late_ref, outs, held, sems = refs
     copies = []
 
     def intra(kind, h):
-        for ref, jobs in ((first_ref, BESIDE_FIRST), (groups_ref, BESIDE_GROUPS), (extra_ref, EXTRA)):
+        for ref, jobs in ((first_ref, BESIDE_FIRST), (groups_ref, BESIDE_GROUPS)):
             if (kind, h) in jobs:
                 i = jobs.index((kind, h))
                 return ref[:, i * HEAD_DIM : (i + 1) * HEAD_DIM]
+        i = EXTRA.index((kind, h))
+        cols = slice(i * HEAD_DIM, (i + 1) * HEAD_DIM)
+        return jnp.where(early(), soon_ref[:, cols], late_ref[:, cols])
 
     cosine = cos_ref[...] * scale
     sine = sin_ref[...] * scale
@@ -266,7 +269,7 @@
 
 
 def own_kernel(chip_ref, *refs, scale):
-    refs = (*refs[:8], refs[8:11], refs[11:14], refs[14])
+    refs = (*refs[:9], refs[9:12], refs[12:15], refs[15])
     keys_here = on_keys()
 
     @pl.when(keys_here)
@@ -279,7 +282,7 @@
 
 
 def final_kernel(came_ref, *refs, scale):
-    refs = (*refs[:8], refs[11:14], refs[14:17], refs[17])
+    refs = (*refs[:9], refs[12:15], refs[15:18], refs[18])
     keys_here = on_keys()
 
     @pl.when(keys_here)
@@ -338,7 +341,7 @@
     piece = (WIDTH // chips, HEAD_DIM)
     came = lax.ppermute(other, "stretch", swap)
     rows = (qr, kr, v, o)
-    first, extra = call(
+    first, soon = call(
         first_kernel, products(BESIDE_FIRST, EXTRA), [WHOLE] * 4, work(BESIDE_FIRST)
     )(*rows)
     (pair,) = call(pair_kernel, [(state, F32)], [WHOLE] * 3, (0, 1 << 19))(mine, came, first)
@@ -356,9 +359,9 @@
     chip = lax.all_to_all(place, "stretch", 0, 0, axis_index_groups=GROUPS).reshape(state)
     own_state, sent = call(own_state_kernel, [(state, F32)] * 2, [WHOLE] * 3, (0, 1 << 19))(chip, mine, came)
     came = lax.ppermute(sent, "stretch", swap)
-    (extra,) = call(
-        last_kernel, products(EXTRA), [WHOLE] * 6, work(EXTRA), aliases={5: 0}
-    )(*rows, chip, extra)
+    (late,) = call(
+        last_kernel, products(EXTRA), [WHOLE] * 5, work(EXTRA)
+    )(*rows, chip)
 
     def own(*refs):
         own_kernel(*refs, scale=scale)
@@ -367,12 +370,12 @@
         final_kernel(*refs, scale=scale)
 
     held = [pltpu.VMEM(wide, BF16)] * 3 + [pltpu.SemaphoreType.DMA((2 * HEADS,))]
-    common = (kr, v, o, cosine, sine, first, groups, extra)
+    common = (kr, v, o, cosine, sine, first, groups, soon, late)
     cost = (2 * 4 * 2 * 512 * 128 * 128, 4 << 20)
-    begun = call(own, [(wide, BF16)] * 3, [WHOLE] * 9, cost, out_spec=HBM, scratch=held)(own_state, *common)
+    begun = call(own, [(wide, BF16)] * 3, [WHOLE] * 10, cost, out_spec=HBM, scratch=held)(own_state, *common)
     return call(
-        final, [(wide, BF16)] * 3, [WHOLE] * 9 + [HBM] * 3, cost, out_spec=HBM, scratch=held,
-        aliases={9: 0, 10: 1, 11: 2},
+        final, [(wide, BF16)] * 3, [WHOLE] * 10 + [HBM] * 3, cost, out_spec=HBM, scratch=held,
+        aliases={10: 0, 11: 1, 12: 2},
     )(came, *common, *begun)
 
 

time: 52.7 us -> 52.9 us (level)
  no operation moved by 1% of the time
where the time goes in v6:
time: 52.9 us; the launch traced here: 52.7 us
  blocking collectives  29.5 us (56%)
  Pallas kernels  10.8 us (20%)
  starting transfers between devices  10.7 us (20%)
  waiting for transfers between devices  0.96 us (2%)
  between operations  0.72 us (1%)
    all_to_all x1, blocking collectives, shards(): lax.all_to_all(pair.reshape((chips,) + piece), 'stretch', 0, 0, axis_inde...  15.8 us
    all_to_all x1, blocking collectives, shards(): lax.all_to_all(place, 'stretch', 0, 0, axis_index_groups=GROUPS)  13.8 us
    ppermute x3, starting transfers between devices, shards(): lax.ppermute(total, 'grp', [(i, i ^ step) for i in range(ny)])  3.79 us
    ppermute x1, starting transfers between devices, shards(): came = lax.ppermute(sent, 'stretch', swap)  3.54 us
    ppermute x1, starting transfers between devices, shards(): came = lax.ppermute(other, 'stretch', swap)  3.33 us
    pallas_call x1, Pallas kernels, shards(): call(first_kernel, products(BESIDE_FIRST, EXTRA), [WHOLE] * 4, work(BESID...  3.03 us
    pallas_call x1, Pallas kernels, shards(): call(rotate_kernel, [(wide, BF16)] * 4 + [(table, F32)] * 2 + [(state, F3...  2.72 us
    pallas_call x1, Pallas kernels, shards(): call(groups_kernel, products(BESIDE_GROUPS), [WHOLE] * 5, work(BESIDE_GRO...  1.97 us
  transfers between devices with their start and end apart: 5, of which 1 were waited for; matrix products, arithmetic and copies ran while one was open for 0% of the time, Pallas kernels for 12%

profile of v6, /device:TPU:1, one launch (start us, length us, event | category | flops | bytes accessed | tf_op | source)
XLA Modules:
  0.0 52.7 jit_solution(15040487539992619520)
XLA Ops:
  0.6 2.7 %shard_map.85 = (bf16[512,512]{1,0:T(8,128)(2,1)S(1)}, bf16[512,512]{1,0:T(8,128)(2,1)S(1)}, bf16[512,512]{1,0:T(8,128)(2,1)S(1)}, bf16[512,512]{1,0:T(8,128)(2,...) custom-call(s32[4,128]{1,0:T(4,128)} %bitcast.6, ...), custom_call_target="tpu_custom_call" | custom-call | flops 134217728 | bytes 4194304 | tf_op jit(solution)/shard_map/pallas_call | solution.py:315
  3.4 3.3 %collective-permute-start = (f32[512,128]{1,0:T(8,128)S(1)}, f32[512,128]{1,0:T(8,128)S(1)}, u32[]{:S(2)}, u32[]{:S(2)}) collective-permute-start(f32[512,128]{1,0:T(8,128)S(1)} %get-tuple-element.21), channel_id=1, source_target_pairs={{0,1},{1,0},{2,3},{3,2},{4,5},{5,4},{6,7},{7,6},{8,9},{9,8},{10,11... | collective-permute-start | bytes 786440 | tf_op jit(solution)/shard_map/ppermute | solution.py:342
  6.7 3.0 %shard_map.86 = (f32[512,384]{1,0:T(8,128)S(1)}, f32[512,512]{1,0:T(8,128)S(1)}) custom-call(bf16[512,512]{1,0:T(8,128)(2,1)S(1)} %get-tuple-element.22.refs_0_, bf16[512,512]{1,0:T(8,128)(2,1)S(1)} %get-tuple-element.23.refs_1_, bf16[512,512]{1,0:T(8,128)(2,1)S(1)} %get-tuple-element.24.refs_2_, bf16[512,512]{1,0:T(8,128)(2,1)S(1)} %get-tuple-element.25.refs_3_), custom_call_target="tpu_custom_call" | custom-call | flops 402653184 | bytes 3145728 | tf_op jit(solution)/shard_map/pallas_call | solution.py:344
  9.7 0.0 collective-permute-done.came_ref
  9.8 15.8 %all_to_all.10.r_ref = f32[32,16,128]{2,1,0:T(8,128)S(1)} all-to-all(f32[32,16,128]{2,1,0:T(8,128)S(1)} %bitcast.5), channel_id=1, replica_groups={{37,38,40,42,44,46,48,50,52,54,56,58,60,62,0,2,4,6,8,10,12,14,16,18,20,..., dimensions={0} | all-to-all | bytes 524288 | tf_op jit(solution)/shard_map/all_to_all | solution.py:348
  25.5 0.1 shard_map.88
  25.6 3.0 %collective-permute-start.3 = (f32[16,128]{1,0:T(8,128)S(1)}, f32[16,128]{1,0:T(8,128)S(1)}, u32[]{:S(2)}, u32[]{:S(2)}) collective-permute-start(f32[16,128]{1,0:T(8,128)S(1)} %get-tuple-element.28.refs_4_), channel_id=1, source_target_pairs={{0,128},{64,192},{128,0},{192,64},{1,129},{65,193},{129,1},{193,65... | collective-permute-start | bytes 24584 | tf_op jit(solution)/shard_map/ppermute | solution.py:355
  28.6 0.8 %collective-permute-start.2 = (f32[16,128]{1,0:T(8,128)S(1)}, f32[16,128]{1,0:T(8,128)S(1)}, u32[]{:S(2)}, u32[]{:S(2)}) collective-permute-start(f32[16,128]{1,0:T(8,128)S(1)} %get-tuple-element.28.refs_4_), channel_id=1, source_target_pairs={{0,192},{64,128},{128,64},{192,0},{1,193},{65,129},{129,65},{193,1... | collective-permute-start | bytes 24584 | tf_op jit(solution)/shard_map/ppermute | solution.py:355
  29.4 0.0 collective-permute-start.1
  29.4 2.0 %shard_map.89._.refs_7_ = f32[512,640]{1,0:T(8,128)S(1)} custom-call(bf16[512,512]{1,0:T(8,128)(2,1)S(1)} %get-tuple-element.22.refs_0_, bf16[512,512]{1,0:T(8,128)(2,1)S(1)} %get-tuple-element.23.refs_1_, bf16[512,512]{1,0:T(8,128)(2,1)S(1)} %get-tuple-element.24.refs_2_, bf16[512,512]{1,0:T(8,128)(2,1)S(1)} %get-tuple-element.25.refs_3_, ...), custom_call_target="tpu_custom_call" | custom-call | flops 671088640 | bytes 3145728 | tf_op jit(solution)/shard_map/pallas_call | solution.py:352
  31.4 0.0 collective-permute-done.3.c_ref
  31.4 0.9 %collective-permute-done.2.b_ref = f32[16,128]{1,0:T(8,128)S(1)} collective-permute-done((f32[16,128]{1,0:T(8,128)S(1)}, f32[16,128]{1,0:T(8,128)S(1)}, u32[]{:S(2)}, u32[]{:S(2)}) %collective-permute-start.2) | collective-permute-done | bytes 8224 | tf_op jit(solution)/shard_map/ppermute | solution.py:355
  32.3 0.0 collective-permute-done.1.a_ref
  32.4 13.8 %all_to_all.11 = f32[32,16,128]{2,1,0:T(8,128)S(1)} all-to-all(f32[32,16,128]{2,1,0:T(8,128)S(1)} %shard_map.90), channel_id=1, replica_groups={{37,38,40,42,44,46,48,50,52,54,56,58,60,62,0,2,4,6,8,10,12,14,16,18,20,..., dimensions={0} | all-to-all | bytes 524288 | tf_op jit(solution)/shard_map/all_to_all | solution.py:359
  46.2 0.1 shard_map.91
  46.2 3.5 %collective-permute-start.4 = (f32[512,128]{1,0:T(8,128)S(1)}, f32[512,128]{1,0:T(8,128)S(1)}, u32[]{:S(2)}, u32[]{:S(2)}) collective-permute-start(f32[512,128]{1,0:T(8,128)S(1)} %get-tuple-element.29), channel_id=1, source_target_pairs={{0,1},{1,0},{2,3},{3,2},{4,5},{5,4},{6,7},{7,6},{8,9},{9,8},{10,11... | collective-permute-start | bytes 786440 | tf_op jit(solution)/shard_map/ppermute | solution.py:361
  49.8 1.5 %shard_map.93 = (bf16[512,512]{1,0:T(8,128)(2,1)}, bf16[512,512]{1,0:T(8,128)(2,1)}, bf16[512,512]{1,0:T(8,128)(2,1)}) custom-call(f32[512,128]{1,0:T(8,128)S(1)} %get-tuple-element.33.refs_0_, bf16[512,512]{1,0:T(8,128)(2,1)S(1)} %get-tuple-element.23.refs_1_, bf16[512,512]{1,0:T(8,128)(2,1)S(1)} %get-tuple-element.24.refs_2_, ...), custom_call_target="tpu_custom_call" | custom-call | flops 134217728 | bytes 4194304 | tf_op jit(solution)/shard_map/pallas_call | solution.py:375
  51.3 0.0 collective-permute-done.4.refs_0_
  51.3 1.4 %shard_map.94 = (bf16[512,512]{1,0:T(8,128)(2,1)}, bf16[512,512]{1,0:T(8,128)(2,1)}, bf16[512,512]{1,0:T(8,128)(2,1)}) custom-call(f32[512,128]{1,0:T(8,128)S(1)} %collective-permute-done.4.refs_0_, bf16[512,512]{1,0:T(8,128)(2,1)S(1)} %get-tuple-element.23.refs_1_, ...), custom_call_target="tpu_custom_call", output_to_operand_aliasing={{0}: (10, {}), {1}: (11, {}), {2}: (12, {})} | custom-call | flops 134217728 | bytes 4194304 | tf_op jit(solution)/shard_map/pallas_call | solution.py:376
  (3 shorter events, 0.1 us)
Async XLA Ops:
  3.4 6.4 %collective-permute-start = (f32[512,128]{1,0:T(8,128)S(1)}, f32[512,128]{1,0:T(8,128)S(1)}, u32[]{:S(2)}, u32[]{:S(2)}) collective-permute-start(f32[512,128]{1,0:T(8,128)S(1)} %get-tuple-element.21), channel_id=1, source_target_pairs={{0,1},{1,0},{2,3},{3,2},{4,5},{5,4},{6,7},{7,6},{8,9},{9,8},{10,11... | collective-permute-start | bytes 786440 | tf_op jit(solution)/shard_map/ppermute | solution.py:342
  25.6 5.8 %collective-permute-start.3 = (f32[16,128]{1,0:T(8,128)S(1)}, f32[16,128]{1,0:T(8,128)S(1)}, u32[]{:S(2)}, u32[]{:S(2)}) collective-permute-start(f32[16,128]{1,0:T(8,128)S(1)} %get-tuple-element.28.refs_4_), channel_id=1, source_target_pairs={{0,128},{64,192},{128,0},{192,64},{1,129},{65,193},{129,1},{193,65... | collective-permute-start | bytes 24584 | tf_op jit(solution)/shard_map/ppermute | solution.py:355
  28.6 3.7 %collective-permute-start.2 = (f32[16,128]{1,0:T(8,128)S(1)}, f32[16,128]{1,0:T(8,128)S(1)}, u32[]{:S(2)}, u32[]{:S(2)}) collective-permute-start(f32[16,128]{1,0:T(8,128)S(1)} %get-tuple-element.28.refs_4_), channel_id=1, source_target_pairs={{0,192},{64,128},{128,64},{192,0},{1,193},{65,129},{129,65},{193,1... | collective-permute-start | bytes 24584 | tf_op jit(solution)/shard_map/ppermute | solution.py:355
  29.4 2.9 %collective-permute-start.1 = (f32[16,128]{1,0:T(8,128)S(1)}, f32[16,128]{1,0:T(8,128)S(1)}, u32[]{:S(2)}, u32[]{:S(2)}) collective-permute-start(f32[16,128]{1,0:T(8,128)S(1)} %get-tuple-element.28.refs_4_), channel_id=1, source_target_pairs={{0,64},{64,0},{128,192},{192,128},{1,65},{65,1},{129,193},{193,129... | collective-permute-start | bytes 24584 | tf_op jit(solution)/shard_map/ppermute | solution.py:355
  46.2 5.1 %collective-permute-start.4 = (f32[512,128]{1,0:T(8,128)S(1)}, f32[512,128]{1,0:T(8,128)S(1)}, u32[]{:S(2)}, u32[]{:S(2)}) collective-permute-start(f32[512,128]{1,0:T(8,128)S(1)} %get-tuple-element.29), channel_id=1, source_target_pairs={{0,1},{1,0},{2,3},{3,2},{4,5},{5,4},{6,7},{7,6},{8,9},{9,8},{10,11... | collective-permute-start | bytes 786440 | tf_op jit(solution)/shard_map/ppermute | solution.py:361

commit v7 on v6

--- a/solution.py
+++ b/solution.py
@@ -167,7 +167,7 @@
 
 
 def early():
-    return lax.axis_index("stretch") < len(ORDER[0]) // 2
+    return jnp.logical_or(lax.axis_index("stretch") < len(ORDER[0]) // 2, lax.axis_index("grp") == 0)
 
 
 def first_kernel(*refs):

time: 52.9 us -> 52.9 us (level)
  blocking collectives: 29.5 us -> 31.8 us
  starting transfers between devices: 10.7 us -> 9.18 us
  waiting for transfers between devices: 0.96 us -> 0.27 us
    all_to_all x1, blocking collectives: 15.8 us -> 17.5 us  [shards(): lax.all_to_all(pair.reshape((chips,) + piece), 'stretch', 0, 0, axis_inde...]
    ppermute x3, starting transfers between devices: 3.79 us -> 2.74 us  [shards(): lax.ppermute(total, 'grp', [(i, i ^ step) for i in range(ny)])]
    ppermute x3, waiting for transfers between devices: 0.95 us -> 0.27 us  [shards(): lax.ppermute(total, 'grp', [(i, i ^ step) for i in range(ny)])]
where the time goes in v7:
time: 52.9 us; the launch traced here: 52.7 us
  blocking collectives  31.8 us (60%)
  Pallas kernels  10.8 us (20%)
  starting transfers between devices  9.18 us (17%)
  between operations  0.72 us (1%)
    all_to_all x1, blocking collectives, shards(): lax.all_to_all(pair.reshape((chips,) + piece), 'stretch', 0, 0, axis_inde...  17.5 us
    all_to_all x1, blocking collectives, shards(): lax.all_to_all(place, 'stretch', 0, 0, axis_index_groups=GROUPS)  14.2 us
    ppermute x1, starting transfers between devices, shards(): came = lax.ppermute(other, 'stretch', swap)  3.33 us
    ppermute x1, starting transfers between devices, shards(): came = lax.ppermute(sent, 'stretch', swap)  3.12 us
    pallas_call x1, Pallas kernels, shards(): call(first_kernel, products(BESIDE_FIRST, EXTRA), [WHOLE] * 4, work(BESID...  3.03 us
    ppermute x3, starting transfers between devices, shards(): lax.ppermute(total, 'grp', [(i, i ^ step) for i in range(ny)])  2.74 us
    pallas_call x1, Pallas kernels, shards(): call(rotate_kernel, [(wide, BF16)] * 4 + [(table, F32)] * 2 + [(state, F3...  2.72 us
    pallas_call x1, Pallas kernels, shards(): call(groups_kernel, products(BESIDE_GROUPS), [WHOLE] * 5, work(BESIDE_GRO...  1.95 us
  transfers between devices with their start and end apart: 5, of which 1 were waited for; matrix products, arithmetic and copies ran while one was open for 0% of the time, Pallas kernels for 12%

profile of v7, /device:TPU:1, one launch (start us, length us, event | category | flops | bytes accessed | tf_op | source)
XLA Modules:
  0.0 52.7 jit_solution(10125791444024550918)
XLA Ops:
  0.6 2.7 %shard_map.85 = (bf16[512,512]{1,0:T(8,128)(2,1)S(1)}, bf16[512,512]{1,0:T(8,128)(2,1)S(1)}, bf16[512,512]{1,0:T(8,128)(2,1)S(1)}, bf16[512,512]{1,0:T(8,128)(2,...) custom-call(s32[4,128]{1,0:T(4,128)} %bitcast.6, ...), custom_call_target="tpu_custom_call" | custom-call | flops 134217728 | bytes 4194304 | tf_op jit(solution)/shard_map/pallas_call | solution.py:315
  3.4 3.3 %collective-permute-start = (f32[512,128]{1,0:T(8,128)S(1)}, f32[512,128]{1,0:T(8,128)S(1)}, u32[]{:S(2)}, u32[]{:S(2)}) collective-permute-start(f32[512,128]{1,0:T(8,128)S(1)} %get-tuple-element.21), channel_id=1, source_target_pairs={{0,1},{1,0},{2,3},{3,2},{4,5},{5,4},{6,7},{7,6},{8,9},{9,8},{10,11... | collective-permute-start | bytes 786440 | tf_op jit(solution)/shard_map/ppermute | solution.py:342
  6.7 3.0 %shard_map.86 = (f32[512,384]{1,0:T(8,128)S(1)}, f32[512,512]{1,0:T(8,128)S(1)}) custom-call(bf16[512,512]{1,0:T(8,128)(2,1)S(1)} %get-tuple-element.22.refs_0_, bf16[512,512]{1,0:T(8,128)(2,1)S(1)} %get-tuple-element.23.refs_1_, bf16[512,512]{1,0:T(8,128)(2,1)S(1)} %get-tuple-element.24.refs_2_, bf16[512,512]{1,0:T(8,128)(2,1)S(1)} %get-tuple-element.25.refs_3_), custom_call_target="tpu_custom_call" | custom-call | flops 402653184 | bytes 3145728 | tf_op jit(solution)/shard_map/pallas_call | solution.py:344
  9.7 0.0 collective-permute-done.came_ref
  9.8 17.5 %all_to_all.10.r_ref = f32[32,16,128]{2,1,0:T(8,128)S(1)} all-to-all(f32[32,16,128]{2,1,0:T(8,128)S(1)} %bitcast.5), channel_id=1, replica_groups={{37,38,40,42,44,46,48,50,52,54,56,58,60,62,0,2,4,6,8,10,12,14,16,18,20,..., dimensions={0} | all-to-all | bytes 524288 | tf_op jit(solution)/shard_map/all_to_all | solution.py:348
  27.3 0.1 shard_map.88
  27.4 1.3 %collective-permute-start.3 = (f32[16,128]{1,0:T(8,128)S(1)}, f32[16,128]{1,0:T(8,128)S(1)}, u32[]{:S(2)}, u32[]{:S(2)}) collective-permute-start(f32[16,128]{1,0:T(8,128)S(1)} %get-tuple-element.28.refs_4_), channel_id=1, source_target_pairs={{0,128},{64,192},{128,0},{192,64},{1,129},{65,193},{129,1},{193,65... | collective-permute-start | bytes 24584 | tf_op jit(solution)/shard_map/ppermute | solution.py:355
  28.6 0.8 %collective-permute-start.2 = (f32[16,128]{1,0:T(8,128)S(1)}, f32[16,128]{1,0:T(8,128)S(1)}, u32[]{:S(2)}, u32[]{:S(2)}) collective-permute-start(f32[16,128]{1,0:T(8,128)S(1)} %get-tuple-element.28.refs_4_), channel_id=1, source_target_pairs={{0,192},{64,128},{128,64},{192,0},{1,193},{65,129},{129,65},{193,1... | collective-permute-start | bytes 24584 | tf_op jit(solution)/shard_map/ppermute | solution.py:355
  29.4 0.7 %collective-permute-start.1 = (f32[16,128]{1,0:T(8,128)S(1)}, f32[16,128]{1,0:T(8,128)S(1)}, u32[]{:S(2)}, u32[]{:S(2)}) collective-permute-start(f32[16,128]{1,0:T(8,128)S(1)} %get-tuple-element.28.refs_4_), channel_id=1, source_target_pairs={{0,64},{64,0},{128,192},{192,128},{1,65},{65,1},{129,193},{193,129... | collective-permute-start | bytes 24584 | tf_op jit(solution)/shard_map/ppermute | solution.py:355
  30.1 2.0 %shard_map.89._.refs_7_ = f32[512,640]{1,0:T(8,128)S(1)} custom-call(bf16[512,512]{1,0:T(8,128)(2,1)S(1)} %get-tuple-element.22.refs_0_, bf16[512,512]{1,0:T(8,128)(2,1)S(1)} %get-tuple-element.23.refs_1_, bf16[512,512]{1,0:T(8,128)(2,1)S(1)} %get-tuple-element.24.refs_2_, bf16[512,512]{1,0:T(8,128)(2,1)S(1)} %get-tuple-element.25.refs_3_, ...), custom_call_target="tpu_custom_call" | custom-call | flops 671088640 | bytes 3145728 | tf_op jit(solution)/shard_map/pallas_call | solution.py:352
  32.1 0.0 collective-permute-done.3.c_ref
  32.1 0.3 collective-permute-done.2.b_ref
  32.3 0.0 collective-permute-done.1.a_ref
  32.4 14.2 %all_to_all.11 = f32[32,16,128]{2,1,0:T(8,128)S(1)} all-to-all(f32[32,16,128]{2,1,0:T(8,128)S(1)} %shard_map.90), channel_id=1, replica_groups={{37,38,40,42,44,46,48,50,52,54,56,58,60,62,0,2,4,6,8,10,12,14,16,18,20,..., dimensions={0} | all-to-all | bytes 524288 | tf_op jit(solution)/shard_map/all_to_all | solution.py:359
  46.6 0.1 shard_map.91
  46.7 3.1 %collective-permute-start.4 = (f32[512,128]{1,0:T(8,128)S(1)}, f32[512,128]{1,0:T(8,128)S(1)}, u32[]{:S(2)}, u32[]{:S(2)}) collective-permute-start(f32[512,128]{1,0:T(8,128)S(1)} %get-tuple-element.29), channel_id=1, source_target_pairs={{0,1},{1,0},{2,3},{3,2},{4,5},{5,4},{6,7},{7,6},{8,9},{9,8},{10,11... | collective-permute-start | bytes 786440 | tf_op jit(solution)/shard_map/ppermute | solution.py:361
  49.8 1.5 %shard_map.93 = (bf16[512,512]{1,0:T(8,128)(2,1)}, bf16[512,512]{1,0:T(8,128)(2,1)}, bf16[512,512]{1,0:T(8,128)(2,1)}) custom-call(f32[512,128]{1,0:T(8,128)S(1)} %get-tuple-element.33.refs_0_, bf16[512,512]{1,0:T(8,128)(2,1)S(1)} %get-tuple-element.23.refs_1_, bf16[512,512]{1,0:T(8,128)(2,1)S(1)} %get-tuple-element.24.refs_2_, ...), custom_call_target="tpu_custom_call" | custom-call | flops 134217728 | bytes 4194304 | tf_op jit(solution)/shard_map/pallas_call | solution.py:375
  51.3 0.0 collective-permute-done.4.refs_0_
  51.4 1.4 %shard_map.94 = (bf16[512,512]{1,0:T(8,128)(2,1)}, bf16[512,512]{1,0:T(8,128)(2,1)}, bf16[512,512]{1,0:T(8,128)(2,1)}) custom-call(f32[512,128]{1,0:T(8,128)S(1)} %collective-permute-done.4.refs_0_, bf16[512,512]{1,0:T(8,128)(2,1)S(1)} %get-tuple-element.23.refs_1_, ...), custom_call_target="tpu_custom_call", output_to_operand_aliasing={{0}: (10, {}), {1}: (11, {}), {2}: (12, {})} | custom-call | flops 134217728 | bytes 4194304 | tf_op jit(solution)/shard_map/pallas_call | solution.py:376
  (3 shorter events, 0.1 us)
Async XLA Ops:
  3.4 6.4 %collective-permute-start = (f32[512,128]{1,0:T(8,128)S(1)}, f32[512,128]{1,0:T(8,128)S(1)}, u32[]{:S(2)}, u32[]{:S(2)}) collective-permute-start(f32[512,128]{1,0:T(8,128)S(1)} %get-tuple-element.21), channel_id=1, source_target_pairs={{0,1},{1,0},{2,3},{3,2},{4,5},{5,4},{6,7},{7,6},{8,9},{9,8},{10,11... | collective-permute-start | bytes 786440 | tf_op jit(solution)/shard_map/ppermute | solution.py:342
  27.4 4.7 %collective-permute-start.3 = (f32[16,128]{1,0:T(8,128)S(1)}, f32[16,128]{1,0:T(8,128)S(1)}, u32[]{:S(2)}, u32[]{:S(2)}) collective-permute-start(f32[16,128]{1,0:T(8,128)S(1)} %get-tuple-element.28.refs_4_), channel_id=1, source_target_pairs={{0,128},{64,192},{128,0},{192,64},{1,129},{65,193},{129,1},{193,65... | collective-permute-start | bytes 24584 | tf_op jit(solution)/shard_map/ppermute | solution.py:355
  28.6 3.7 %collective-permute-start.2 = (f32[16,128]{1,0:T(8,128)S(1)}, f32[16,128]{1,0:T(8,128)S(1)}, u32[]{:S(2)}, u32[]{:S(2)}) collective-permute-start(f32[16,128]{1,0:T(8,128)S(1)} %get-tuple-element.28.refs_4_), channel_id=1, source_target_pairs={{0,192},{64,128},{128,64},{192,0},{1,193},{65,129},{129,65},{193,1... | collective-permute-start | bytes 24584 | tf_op jit(solution)/shard_map/ppermute | solution.py:355
  29.4 2.9 %collective-permute-start.1 = (f32[16,128]{1,0:T(8,128)S(1)}, f32[16,128]{1,0:T(8,128)S(1)}, u32[]{:S(2)}, u32[]{:S(2)}) collective-permute-start(f32[16,128]{1,0:T(8,128)S(1)} %get-tuple-element.28.refs_4_), channel_id=1, source_target_pairs={{0,64},{64,0},{128,192},{192,128},{1,65},{65,1},{129,193},{193,129... | collective-permute-start | bytes 24584 | tf_op jit(solution)/shard_map/ppermute | solution.py:355
  46.7 4.6 %collective-permute-start.4 = (f32[512,128]{1,0:T(8,128)S(1)}, f32[512,128]{1,0:T(8,128)S(1)}, u32[]{:S(2)}, u32[]{:S(2)}) collective-permute-start(f32[512,128]{1,0:T(8,128)S(1)} %get-tuple-element.29), channel_id=1, source_target_pairs={{0,1},{1,0},{2,3},{3,2},{4,5},{5,4},{6,7},{7,6},{8,9},{9,8},{10,11... | collective-permute-start | bytes 786440 | tf_op jit(solution)/shard_map/ppermute | solution.py:361
